TPU v7x, 512 devices: a whole 4x8x8 slice. The times are simulated.
512 devices in a mesh: grp: 64 (over z_lo, y, core), kv: 8 (over x, z_hi).
Axes of the slice: x: 4, y: 8, z: 8 (z_hi: 2, z_lo: 4; z = z_hi * 4 + z_lo), core: 2. Of those that a mesh axis runs over, the one named last changes fastest.
Arguments:
- query: bfloat16 [16384, 8192], P('grp', 'kv'), may hold values from -6 to 6
- cont_kv: bfloat16 [16384, 2048], P('grp', 'kv'), may hold values from -6 to 6
- prompt_kv: bfloat16 [64, 1024, 2048], P('grp', None, 'kv'), may hold values from -6 to 6
- out_grad: bfloat16 [16384, 8192], P('grp', 'kv'), may hold values from -6 to 6
- lengths: int32 [64], P('grp'), may hold values from 1 to 256, 10240 in all
- owners: int32 [8], P('kv'), may hold values from 0 to 63
Outputs:
- grad_query: bfloat16 [16384, 8192], P(('grp', 'kv'))
- grad_cont_kv: bfloat16 [16384, 2048], P(('grp', 'kv'))
- grad_prompt_kv: bfloat16 [64, 1024, 2048], P('grp', None, 'kv')
Inputs may be any that keep to these rules, and one draw needn't show every extreme that they name: `lengths`: one continuation has exactly 256 live tokens.
All inputs are finite; a program needn't handle non-finite values. No bound on the sum of `lengths` on one device may be relied on, other than what follows from the above.
Results may differ from a plain program's by a relative error of at most 0.0077.
Values may be sent and summed in bfloat16 or wider, within the bound.
No kernel may reach another device: no remote copies, remote signals or barrier semaphores. Data moves between devices by JAX's collectives and lax.ppermute only.
A program may use at most 64 MiB of HBM per device.

v0:
```python
import math

import jax
import jax.numpy as jnp
from jax import lax
from jax.sharding import PartitionSpec as P

WIN = 128


def broadcast(block, axis, source):
    block = jnp.where(lax.axis_index(axis) == source, block, jnp.zeros_like(block))
    return lax.psum(block, axis)


def window_grads(q_rows, d_rows, keys, values, first, prompt_len, length, per_kv):
    head_dim = keys.shape[1]
    width = q_rows.shape[0] // per_kv
    scale = 1.0 / math.sqrt(head_dim)
    scores = (
        lax.dot_general(q_rows, keys, (((1,), (1,)), ((), ())), preferred_element_type=jnp.float32)
        * scale
    )
    position = first + lax.broadcasted_iota(jnp.int32, (q_rows.shape[0], 1), 0) % width
    key_index = lax.broadcasted_iota(jnp.int32, (1, keys.shape[0]), 1)
    allowed = (key_index < prompt_len) | (key_index - prompt_len <= position)
    scores = jnp.where(allowed, scores, -1e30)
    top = jnp.max(scores, axis=-1, keepdims=True)
    expo = jnp.exp(scores - top)
    probs = expo / jnp.sum(expo, axis=-1, keepdims=True)
    weights = probs.astype(jnp.bfloat16)
    attended = jnp.dot(weights, values, preferred_element_type=jnp.float32)
    live_grad = jnp.where(position < length, d_rows, jnp.zeros((), jnp.bfloat16))
    delta = jnp.sum(live_grad.astype(jnp.float32) * attended, axis=-1, keepdims=True)
    prob_grad = lax.dot_general(
        live_grad, values, (((1,), (1,)), ((), ())), preferred_element_type=jnp.float32
    )
    score_grad = (probs * (prob_grad - delta) * scale).astype(jnp.bfloat16)
    grad_q = jnp.dot(score_grad, keys, preferred_element_type=jnp.float32)
    grad_keys = lax.dot_general(
        score_grad, q_rows, (((0,), (0,)), ((), ())), preferred_element_type=jnp.float32
    )
    grad_values = lax.dot_general(
        weights, live_grad, (((0,), (0,)), ((), ())), preferred_element_type=jnp.float32
    )
    grad_q = (
        grad_q.reshape(per_kv, width, head_dim).transpose(1, 0, 2).reshape(width, per_kv * head_dim)
    )
    return (grad_q.astype(jnp.bfloat16), jnp.concatenate([grad_keys, grad_values], 1))


def head_major(block, per_kv, head_dim):
    width = block.shape[0]
    return (
        block.reshape(width, per_kv, head_dim).transpose(1, 0, 2).reshape(per_kv * width, head_dim)
    )


def body(query, cont_kv, prompt_kv, out_grad, lengths, owners):
    head_dim = cont_kv.shape[1] // 2
    seq_rows = query.shape[0]
    per_kv = query.shape[1] // head_dim
    prompt_len = prompt_kv.shape[1]
    root = owners[0]
    length = lengths[0]
    shared = broadcast(prompt_kv[0], "grp", root)
    keys = jnp.concatenate([shared[:, :head_dim], cont_kv[:, :head_dim]], 0)
    values = jnp.concatenate([shared[:, head_dim:], cont_kv[:, head_dim:]], 0)
    total = jnp.zeros((prompt_len + seq_rows, 2 * head_dim), jnp.float32)
    grad_blocks = []
    for window in range(seq_rows // WIN):
        first = window * WIN
        span = prompt_len + first + WIN
        q_rows = head_major(query[first : first + WIN], per_kv, head_dim)
        d_rows = head_major(out_grad[first : first + WIN], per_kv, head_dim)

        def active(q_part, d_part, key_part, value_part, first=first):
            return window_grads(
                q_part, d_part, key_part, value_part, first, prompt_len, length, per_kv
            )

        def skipped(q_part, d_part, key_part, value_part):
            return (
                jnp.zeros((q_part.shape[0] // per_kv, per_kv * head_dim), jnp.bfloat16),
                jnp.zeros((key_part.shape[0], 2 * head_dim), jnp.float32),
            )

        grad_q, grad_both = lax.cond(
            first < length, active, skipped, q_rows, d_rows, keys[:span], values[:span]
        )
        grad_blocks.append(grad_q)
        total = total.at[:span].add(grad_both)
    grad_query = jnp.concatenate(grad_blocks, 0)
    grad_cont = total[prompt_len:].astype(jnp.bfloat16)
    prompt_terms = total[:prompt_len]
    token_query, token_cont = (
        lax.all_to_all(grad_query, "kv", split_axis=0, concat_axis=1, tiled=True),
        lax.all_to_all(grad_cont, "kv", split_axis=0, concat_axis=1, tiled=True),
    )
    summed = lax.psum(prompt_terms, "grp")
    rounded = summed.astype(jnp.bfloat16)
    mine = lax.axis_index("grp") == root
    grad_prompt = jnp.where(mine, rounded, jnp.zeros((), jnp.bfloat16))
    return (token_query, token_cont, grad_prompt[None])


def solution(mesh):
    placed = (
        P("grp", "kv"),
        P("grp", "kv"),
        P("grp", None, "kv"),
        P("grp", "kv"),
        P("grp"),
        P("kv"),
    )
    return jax.shard_map(
        body,
        mesh=mesh,
        in_specs=placed,
        out_specs=(P(("grp", "kv"), None), P(("grp", "kv"), None), P("grp", None, "kv")),
        check_vma=False,
    )
```

profile of v0, /device:TPU:1, one launch (start us, length us, event | category | flops | bytes accessed | tf_op | source)
XLA Modules:
  0.0 882.5 jit_solution(11485771958665005879)
XLA Ops:
  7.9 0.8 select_bitcast_fusion.1
  8.8 1.1 fusion.46
  10.7 1.1 fusion.45
  11.9 0.8 copy.61
  13.0 538.0 %all-reduce.5.cloned.1.call-done = bf16[1024,256]{1,0:T(8,128)(2,1)} async-done(((bf16[1024,256]{1,0:T(8,128)(2,1)}), bf16[1024,256]{1,0:T(8,128)(2,1)}) %all-reduce.5.cloned.1.call-update) | async-done | bytes 524304 | tf_op jit(solution)/shard_map/psum | solution.py:13
  551.0 1.1 fusion.47
  552.8 12.4 %conditional.3 = (bf16[128,1024]{1,0:T(8,128)(2,1)}, f32[1280,256]{1,0:T(8,128)S(1)}) conditional(s32[]{:T(128)} %convert_element_type.53, () %tuple.41, (bf16[8,128,128]{1,2,0:T(8,128)(2,1)S(1)}, bf16[1280,128]{1,0:T(8,128)(2,1)}, s32[]{:T(128)}, bf16[8,128,128]{1,2,0:T(8,128)(2,1)S(1)}, bf16[1280,128]{1,0:T(8,128)(2,1)S(1)}) %tuple.70), branch_computations={%region_6.7_spmd, %region_7.11_spmd} | conditional | flops 2034186752 | bytes 55104020 | solution.py:88
  553.0 2.5 fusion.44
  555.5 1.1 fusion.24
  556.6 1.4 fusion.23
  558.7 1.0 fusion.32
  559.7 1.3 multiply_convert_fusion
  561.0 1.8 convolution_convert_fusion.1
  562.9 0.8 copy.84
  565.3 14.5 %conditional.2 = (bf16[128,1024]{1,0:T(8,128)(2,1)S(1)}, f32[1280,256]{1,0:T(8,128)S(1)}) conditional(s32[]{:T(128)} %convert_element_type.52, () %tuple.39, (bf16[8,128,128]{1,2,0:T(8,128)(2,1)}, bf16[1280,128]{1,0:T(8,128)(2,1)}, s32[]{:T(128)}, bf16[8,128,128]{1,2,0:T(8,128)(2,1)S(1)}, bf16[1280,128]{1,0:T(8,128)(2,1)S(1)}) %tuple.69), branch_computations={%region_1.2_spmd, %region_2.6_spmd} | conditional | flops 1830859008 | bytes 52350232 | solution.py:88
  565.5 1.1 copy.46
  566.6 2.4 fusion.43
  569.1 1.0 fusion.4
  570.1 1.0 fusion.3
  571.8 0.9 fusion.9
  572.7 1.2 fusion.5
  574.0 1.7 convolution_convert_fusion
  577.0 1.4 copy.60
  578.4 1.4 scatter-add.9.clone
  580.0 1.1 copy-done
  581.7 6.9 all-to-all-start.1
  588.6 1.8 pad_maximum_fusion.2
  590.4 7.7 all-to-all-done.1
  598.1 3.5 all-to-all-start
  601.7 271.7 %all-reduce.6 = bf16[1024,256]{1,0:T(8,128)(2,1)S(1)} all-reduce(f32[1024,256]{1,0:T(8,128)S(1)} %slice-done), channel_id=1, replica_groups=mesh['grp'=64,'kv'=8] {'grp'}, use_global_device_ids=true, to_apply=%region_11.12 | all-reduce | flops 262144 | bytes 1572864 | tf_op jit(solution)/shard_map/psum | solution.py:100
  873.4 0.8 select_bitcast_fusion
  874.9 0.8 copy.69
  (33 shorter events, 7.2 us)
Async XLA Ops:
  7.2 5.8 copy-start.1
  7.2 543.8 %all-reduce.5.cloned.1.call-start = ((), (), s32[]{:S(2)}) async-start(), calls=%async_computation.2 | async-start | bytes 1048576 | tf_op jit(solution)/shard_map/psum | solution.py:13
  579.9 1.1 copy-start
  581.7 20.0 %slice-start = ((f32[1280,256]{1,0:T(8,128)}), f32[1024,256]{1,0:T(8,128)S(1)}, s32[]{:S(2)}) async-start(f32[1280,256]{1,0:T(8,128)} %copy-done), calls=%async_computation.3 | async-start | bytes 2097152 | tf_op jit(solution)/shard_map/slice | solution.py:95
  581.7 16.5 %all-to-all-start.1 = ((bf16[8,32,256]{2,1,0:T(8,128)(2,1)}), bf16[8,32,256]{2,1,0:T(8,128)(2,1)S(1)}, u32[]{:S(2)}, u32[]{:S(2)}) async-start(bf16[8,32,256]{2,1,0:T(8,128)(2,1)} %bitcast.19), calls=%async_computation.1 | async-start | bytes 262144 | tf_op jit(solution)/shard_map/all_to_all | solution.py:98
  598.1 276.7 %all-to-all-start = ((bf16[8,32,1024]{2,1,0:T(8,128)(2,1)}), bf16[8,32,1024]{2,1,0:T(8,128)(2,1)S(1)}, u32[]{:S(2)}, u32[]{:S(2)}) async-start(bf16[8,32,1024]{2,1,0:T(8,128)(2,1)} %bitcast.17), calls=%async_computation | async-start | bytes 1048576 | tf_op jit(solution)/shard_map/all_to_all | solution.py:97
Sparse Core Ops, SparseCore 0:
  11.5 539.4 all-reduce.4
where the time goes:
time: 888 us; the launch traced here: 883 us
  waiting for transfers between devices  546 us (61%)
  blocking collectives  272 us (31%)
  between operations  15.5 us (2%)
  matrix products  15.2 us (2%)
  local copies, waits for them, and re-layouts  13.1 us (1%)
  starting transfers between devices  10.5 us (1%)
  other arithmetic  10.5 us (1%)
    psum x1, waiting for transfers between devices, broadcast(): return lax.psum(block, axis)  538 us
    psum x1, blocking collectives, body(): summed = lax.psum(prompt_terms, 'grp')  272 us
  transfers between devices with their start and end apart: 3, of which 2 were waited for; matrix products, arithmetic and copies ran while one was open for 1% of the time, Pallas kernels for 0%

commit v1 on v0

--- a/solution.py
+++ b/solution.py
@@ -6,11 +6,39 @@
 from jax.sharding import PartitionSpec as P
 
 WIN = 128
+CHIPS = ("zl", "y")
 
 
-def broadcast(block, axis, source):
-    block = jnp.where(lax.axis_index(axis) == source, block, jnp.zeros_like(block))
-    return lax.psum(block, axis)
+def spread(block, root):
+    rows, width = block.shape
+    peers = lax.axis_size(CHIPS)
+    halves = lax.all_to_all(block.reshape(2, rows // 2, width), "core", 0, 0, tiled=True)
+    half = lax.dynamic_index_in_dim(halves, root % 2, 0, keepdims=False)
+    pieces = half.reshape(peers, rows // 2 // peers, width)
+    pieces = lax.all_to_all(pieces, CHIPS, 0, 0, tiled=True)
+    piece = lax.dynamic_index_in_dim(pieces, root // 2, 0, keepdims=True)
+    return collect(piece, rows, width)
+
+
+def collect(piece, rows, width):
+    peers = lax.axis_size(CHIPS)
+    copies = jnp.broadcast_to(piece, (peers, *piece.shape[1:]))
+    half = lax.all_to_all(copies, CHIPS, 0, 0, tiled=True).reshape(rows // 2, width)
+    return lax.all_gather(half, "core", tiled=True)
+
+
+def total_over_group(terms):
+    rows, width = terms.shape
+    peers = lax.axis_size(CHIPS)
+    core = lax.axis_index("core")
+    halves = terms.reshape(2, rows // 2, width)
+    own = lax.dynamic_index_in_dim(halves, core, 0, keepdims=False)
+    other = lax.dynamic_index_in_dim(halves, 1 - core, 0, keepdims=False)
+    half = own + lax.ppermute(other, "core", [(0, 1), (1, 0)])
+    pieces = half.astype(jnp.bfloat16).reshape(peers, rows // 2 // peers, width)
+    pieces = lax.all_to_all(pieces, CHIPS, 0, 0, tiled=True)
+    piece = jnp.sum(pieces.astype(jnp.float32), axis=0, keepdims=True).astype(jnp.bfloat16)
+    return collect(piece, rows, width)
 
 
 def window_grads(q_rows, d_rows, keys, values, first, prompt_len, length, per_kv):
@@ -63,7 +91,7 @@
     prompt_len = prompt_kv.shape[1]
     root = owners[0]
     length = lengths[0]
-    shared = broadcast(prompt_kv[0], "grp", root)
+    shared = spread(prompt_kv[0], root)
     keys = jnp.concatenate([shared[:, :head_dim], cont_kv[:, :head_dim]], 0)
     values = jnp.concatenate([shared[:, head_dim:], cont_kv[:, head_dim:]], 0)
     total = jnp.zeros((prompt_len + seq_rows, 2 * head_dim), jnp.float32)
@@ -97,26 +125,27 @@
         lax.all_to_all(grad_query, "kv", split_axis=0, concat_axis=1, tiled=True),
         lax.all_to_all(grad_cont, "kv", split_axis=0, concat_axis=1, tiled=True),
     )
-    summed = lax.psum(prompt_terms, "grp")
-    rounded = summed.astype(jnp.bfloat16)
-    mine = lax.axis_index("grp") == root
+    rounded = total_over_group(prompt_terms)
+    mine = lax.axis_index(("zl", "y", "core")) == root
     grad_prompt = jnp.where(mine, rounded, jnp.zeros((), jnp.bfloat16))
     return (token_query, token_cont, grad_prompt[None])
 
 
 def solution(mesh):
+    groups = ("zl", "y", "core")
+    fine = jax.sharding.Mesh(mesh.devices.reshape(4, 8, 2, 8), (*groups, "kv"))
     placed = (
-        P("grp", "kv"),
-        P("grp", "kv"),
-        P("grp", None, "kv"),
-        P("grp", "kv"),
-        P("grp"),
+        P(groups, "kv"),
+        P(groups, "kv"),
+        P(groups, None, "kv"),
+        P(groups, "kv"),
+        P(groups),
         P("kv"),
     )
     return jax.shard_map(
         body,
-        mesh=mesh,
+        mesh=fine,
         in_specs=placed,
-        out_specs=(P(("grp", "kv"), None), P(("grp", "kv"), None), P("grp", None, "kv")),
+        out_specs=(P((*groups, "kv"), None), P((*groups, "kv"), None), P(groups, None, "kv")),
         check_vma=False,
     )

time: 888 us -> 166 us (0.19)
  waiting for transfers between devices: 546 us -> 55.6 us
  blocking collectives: 272 us -> 9.84 us
  starting transfers between devices: 10.5 us -> 70.7 us
  between operations: 15.5 us -> 2.19 us
    psum x1 -> x0, waiting for transfers between devices: 538 us -> none  [broadcast(): return lax.psum(block, axis)]
    psum x1 -> x0, blocking collectives: 272 us -> none  [body(): summed = lax.psum(prompt_terms, 'grp')]
    all_to_all x0 -> x5, starting transfers between devices: none -> 43.5 us  [the longest x2 20.2 us: collect(): lax.all_to_all(copies, CHIPS, 0, 0, tiled=True).reshape(rows // 2, width)]
    all_to_all x0 -> x5, waiting for transfers between devices: none -> 35.4 us  [the longest x2 16.3 us: collect(): lax.all_to_all(copies, CHIPS, 0, 0, tiled=True).reshape(rows // 2, width)]
    ppermute x0 -> x1, starting transfers between devices: none -> 13.9 us  [total_over_group(): half = own + lax.ppermute(other, 'core', [(0, 1), (1, 0)])]
    all_to_all x1, waiting for transfers between devices: 0.01 us -> 11.4 us  [body(): lax.all_to_all(grad_query, 'kv', split_axis=0, concat_axis=1, tiled=True)]
    all_gather x0 -> x2, blocking collectives: none -> 9.84 us  [collect(): return lax.all_gather(half, 'core', tiled=True)]
  transfers between devices with their start and end apart: 3 -> 8, of which waited for: 2 -> 7; matrix products, arithmetic and copies ran while one was open for 1% -> 5% of each run, Pallas kernels for 0% -> 0%
where the time goes in v1:
time: 166 us; the launch traced here: 165 us
  starting transfers between devices  70.7 us (43%)
  waiting for transfers between devices  55.6 us (33%)
  local copies, waits for them, and re-layouts  12.1 us (7%)
  blocking collectives  9.84 us (6%)
  matrix products  7.46 us (4%)
  other arithmetic  7.16 us (4%)
  between operations  2.19 us (1%)
    all_to_all x2, starting transfers between devices, collect(): lax.all_to_all(copies, CHIPS, 0, 0, tiled=True).reshape(rows // 2, width)  20.2 us
    all_to_all x2, waiting for transfers between devices, collect(): lax.all_to_all(copies, CHIPS, 0, 0, tiled=True).reshape(rows // 2, width)  16.3 us
    ppermute x1, starting transfers between devices, total_over_group(): half = own + lax.ppermute(other, 'core', [(0, 1), (1, 0)])  13.9 us
    all_to_all x1, waiting for transfers between devices, body(): lax.all_to_all(grad_query, 'kv', split_axis=0, concat_axis=1, tiled=True)  11.4 us
    all_to_all x1, starting transfers between devices, spread(): lax.all_to_all(block.reshape(2, rows // 2, width), 'core', 0, 0, tiled=True)  10.5 us
    all_to_all x1, waiting for transfers between devices, spread(): pieces = lax.all_to_all(pieces, CHIPS, 0, 0, tiled=True)  10.1 us
    all_gather x2, blocking collectives, collect(): return lax.all_gather(half, 'core', tiled=True)  9.84 us
    all_to_all x1, starting transfers between devices, body(): lax.all_to_all(grad_cont, 'kv', split_axis=0, concat_axis=1, tiled=True)  9.76 us
  transfers between devices with their start and end apart: 8, of which 7 were waited for; matrix products, arithmetic and copies ran while one was open for 5% of the time, Pallas kernels for 0%

profile of v1, /device:TPU:1, one launch (start us, length us, event | category | flops | bytes accessed | tf_op | source)
XLA Modules:
  0.0 165.3 jit_solution(16585563874250764822)
XLA Ops:
  0.7 10.5 %all-to-all-start = ((bf16[2,512,256]{2,1,0:T(8,128)(2,1)}), bf16[2,512,256]{2,1,0:T(8,128)(2,1)S(1)}, u32[]{:S(2)}, u32[]{:S(2)}) async-start(bf16[2,512,256]{2,1,0:T(8,128)(2,1)} %bitcast.117), calls=%async_computation | async-start | bytes 1048576 | tf_op jit(solution)/shard_map/all_to_all | solution.py:15
  13.2 7.3 %all-to-all-start.1 = ((bf16[32,16,256]{2,1,0:T(8,128)(2,1)}), bf16[32,16,256]{2,1,0:T(8,128)(2,1)S(1)}, u32[]{:S(2)}, u32[]{:S(2)}) async-start(bf16[32,16,256]{2,1,0:T(8,128)(2,1)} %bitcast.11), calls=%async_computation.1 | async-start | bytes 524288 | tf_op jit(solution)/shard_map/all_to_all | solution.py:18
  20.5 10.1 %all-to-all-done.1 = bf16[32,16,256]{2,1,0:T(8,128)(2,1)S(1)} async-done(((bf16[32,16,256]{2,1,0:T(8,128)(2,1)}), bf16[32,16,256]{2,1,0:T(8,128)(2,1)S(1)}, u32[]{:S(2)}, u32[]{:S(2)}) %all-to-all-start.1) | async-done | bytes 262176 | tf_op jit(solution)/shard_map/all_to_all | solution.py:18
  31.4 6.4 %all-to-all-start.2 = ((bf16[32,16,256]{2,1,0:T(8,128)(2,1)}), bf16[32,16,256]{2,1,0:T(8,128)(2,1)S(1)}, u32[]{:S(2)}, u32[]{:S(2)}) async-start(bf16[32,16,256]{2,1,0:T(8,128)(2,1)} %broadcast_in_dim.55), calls=%async_computation.2 | async-start | bytes 524288 | tf_op jit(solution)/shard_map/all_to_all | solution.py:26
  37.8 1.1 fusion.47
  40.3 7.6 %all-to-all-done.2 = bf16[32,16,256]{2,1,0:T(8,128)(2,1)S(1)} async-done(((bf16[32,16,256]{2,1,0:T(8,128)(2,1)}), bf16[32,16,256]{2,1,0:T(8,128)(2,1)S(1)}, u32[]{:S(2)}, u32[]{:S(2)}) %all-to-all-start.2) | async-done | bytes 262176 | tf_op jit(solution)/shard_map/all_to_all | solution.py:26
  47.9 5.2 %all_gather.6 = bf16[1024,256]{1,0:T(8,128)(2,1)S(1)} all-gather(bf16[512,256]{1,0:T(8,128)(2,1)S(1)} %bitcast.108), channel_id=1, replica_groups=mesh['zl'=4,'y'=8,'core'=2,'kv'=8] {'core'}, dimensions={0}, use_global_device_ids=true | all-gather | bytes 786432 | tf_op jit(solution)/shard_map/all_gather | solution.py:27
  53.9 0.8 conditional.3
  54.7 13.6 %conditional.2 = (bf16[128,1024]{1,0:T(8,128)(2,1)S(1)}, f32[1280,256]{1,0:T(8,128)S(1)}) conditional(s32[]{:T(128)} %convert_element_type.59, () %tuple.39, (bf16[8,128,128]{1,2,0:T(8,128)(2,1)S(1)}, bf16[1280,128]{1,0:T(8,128)(2,1)}, s32[]{:T(128)}, bf16[8,128,128]{1,2,0:T(8,128)(2,1)S(1)}, bf16[1280,128]{1,0:T(8,128)(2,1)S(1)}) %tuple.69), branch_computations={%region_0.1_spmd, %region_1.5_spmd} | conditional | flops 1830859008 | bytes 52350232 | solution.py:116
  55.1 2.4 %fusion.44 = (f32[1024]{0:T(1024)S(1)}, f32[1024,1152]{1,0:T(8,128)S(1)}) fusion(bf16[1024,128]{1,0:T(8,128)(2,1)S(1)} %bitcast.112, bf16[1280,128]{1,0:T(8,128)(2,1)} %get-tuple-element.61, s32[1024]{0:T(1024)S(1)} %add_select_fusion, s32[1152]{0:T(1024)S(1)} %iota_add_fusion, pred[1152]{0:T(1024)(128)(4,1)S(1)} %iota_compare_fusion), kind=kOutput, calls=%fused_computation.72 | convolution fusion | flops 307887104 | bytes 5289600 | tf_op jit(solution)/shard_map/cond/branch_1_fun/dot_general | solution.py:49
  57.5 1.0 fusion.4
  58.6 1.0 fusion.3
  60.3 0.9 fusion.9
  61.2 1.2 fusion.5
  62.4 1.7 %convolution_convert_fusion = bf16[1024,128]{1,0:T(8,128)(2,1)S(1)} fusion(bf16[1024,1152]{1,0:T(8,128)(2,1)S(1)} %fusion.5, bf16[1280,128]{1,0:T(8,128)(2,1)} %get-tuple-element.61), kind=kOutput, calls=%fused_computation.10 | convolution fusion | flops 302120960 | bytes 2916352 | tf_op jit(solution)/shard_map/cond/branch_1_fun/dot_general | solution.py:67
  65.5 1.4 copy.71
  66.9 1.4 scatter-add.9.clone
  68.4 1.1 copy-done
  69.6 13.9 %collective-permute-start = (f32[512,256]{1,0:T(8,128)S(1)}, f32[512,256]{1,0:T(8,128)S(1)}, u32[]{:S(2)}, u32[]{:S(2)}) collective-permute-start(f32[512,256]{1,0:T(8,128)S(1)} %dynamic-slice_bitcast_fusion), channel_id=1, source_target_pairs={{0,8},{8,0},{1,9},{9,1},{2,10},{10,2},{3,11},{11,3},{4,12},{12,4},... | collective-permute-start | bytes 1572872 | tf_op jit(solution)/shard_map/ppermute | solution.py:37
  83.5 1.6 slice.92
  85.1 9.8 %all-to-all-start.4 = ((bf16[8,32,256]{2,1,0:T(8,128)(2,1)}), bf16[8,32,256]{2,1,0:T(8,128)(2,1)S(1)}, u32[]{:S(2)}, u32[]{:S(2)}) async-start(bf16[8,32,256]{2,1,0:T(8,128)(2,1)} %bitcast.22), calls=%async_computation.4 | async-start | bytes 262144 | tf_op jit(solution)/shard_map/all_to_all | solution.py:126
  95.7 8.8 %all-to-all-done.4 = bf16[8,32,256]{2,1,0:T(8,128)(2,1)S(1)} async-done(((bf16[8,32,256]{2,1,0:T(8,128)(2,1)}), bf16[8,32,256]{2,1,0:T(8,128)(2,1)S(1)}, u32[]{:S(2)}, u32[]{:S(2)}) %all-to-all-start.4) | async-done | bytes 131104 | tf_op jit(solution)/shard_map/all_to_all | solution.py:126
  104.5 5.5 %all-to-all-start.5 = ((bf16[32,16,256]{2,1,0:T(8,128)(2,1)}), bf16[32,16,256]{2,1,0:T(8,128)(2,1)S(1)}, u32[]{:S(2)}, u32[]{:S(2)}) async-start(bf16[32,16,256]{2,1,0:T(8,128)(2,1)} %bitcast.27), calls=%async_computation.5 | async-start | bytes 524288 | tf_op jit(solution)/shard_map/all_to_all | solution.py:39
  110.0 1.8 %pad_maximum_fusion.2 = bf16[256,1024]{1,0:T(8,128)(2,1)} fusion(bf16[128,1024]{1,0:T(8,128)(2,1)} %get-tuple-element.78, bf16[128,1024]{1,0:T(8,128)(2,1)S(1)} %get-tuple-element.77), kind=kLoop, calls=%fused_computation.62 | loop fusion | flops 1048576 | bytes 1048576 | tf_op jit(solution)/shard_map/concatenate | solution.py:121
  111.8 8.2 %all-to-all-done.5 = bf16[32,16,256]{2,1,0:T(8,128)(2,1)S(1)} async-done(((bf16[32,16,256]{2,1,0:T(8,128)(2,1)}), bf16[32,16,256]{2,1,0:T(8,128)(2,1)S(1)}, u32[]{:S(2)}, u32[]{:S(2)}) %all-to-all-start.5) | async-done | bytes 262176 | tf_op jit(solution)/shard_map/all_to_all | solution.py:39
  120.0 3.5 %all-to-all-start.3 = ((bf16[8,32,1024]{2,1,0:T(8,128)(2,1)}), bf16[8,32,1024]{2,1,0:T(8,128)(2,1)S(1)}, u32[]{:S(2)}, u32[]{:S(2)}) async-start(bf16[8,32,1024]{2,1,0:T(8,128)(2,1)} %bitcast.20), calls=%async_computation.3 | async-start | bytes 1048576 | tf_op jit(solution)/shard_map/all_to_all | solution.py:125
  123.6 11.4 %all-to-all-done.3 = bf16[8,32,1024]{2,1,0:T(8,128)(2,1)S(1)} async-done(((bf16[8,32,1024]{2,1,0:T(8,128)(2,1)}), bf16[8,32,1024]{2,1,0:T(8,128)(2,1)S(1)}, u32[]{:S(2)}, u32[]{:S(2)}) %all-to-all-start.3) | async-done | bytes 524320 | tf_op jit(solution)/shard_map/all_to_all | solution.py:125
  135.7 13.9 %all-to-all-start.6 = ((bf16[32,16,256]{2,1,0:T(8,128)(2,1)}), bf16[32,16,256]{2,1,0:T(8,128)(2,1)S(1)}, u32[]{:S(2)}, u32[]{:S(2)}) async-start(bf16[32,16,256]{2,1,0:T(8,128)(2,1)} %broadcast_in_dim.56), calls=%async_computation.6 | async-start | bytes 524288 | tf_op jit(solution)/shard_map/all_to_all | solution.py:26
  150.3 0.8 copy.80
  151.1 8.7 %all-to-all-done.6 = bf16[32,16,256]{2,1,0:T(8,128)(2,1)S(1)} async-done(((bf16[32,16,256]{2,1,0:T(8,128)(2,1)}), bf16[32,16,256]{2,1,0:T(8,128)(2,1)S(1)}, u32[]{:S(2)}, u32[]{:S(2)}) %all-to-all-start.6) | async-done | bytes 262176 | tf_op jit(solution)/shard_map/all_to_all | solution.py:26
  159.8 4.7 %all_gather.7 = bf16[1024,256]{1,0:T(8,128)(2,1)S(1)} all-gather(bf16[512,256]{1,0:T(8,128)(2,1)S(1)} %bitcast.109), channel_id=1, replica_groups=mesh['zl'=4,'y'=8,'core'=2,'kv'=8] {'core'}, dimensions={0}, use_global_device_ids=true | all-gather | bytes 786432 | tf_op jit(solution)/shard_map/all_gather | solution.py:27
  164.5 0.8 select_bitcast_fusion
  (36 shorter events, 9.1 us)
Async XLA Ops:
  0.6 39.1 %copy-start.1 = (bf16[256,1024]{1,0:T(8,128)(2,1)S(1)}, bf16[256,1024]{1,0:T(8,128)(2,1)}, u32[]{:S(2)}) copy-start(bf16[256,1024]{1,0:T(8,128)(2,1)} %param.19) | copy-start | bytes 1572868
  0.6 39.6 %copy-start.2 = (bf16[256,256]{1,0:T(8,128)(2,1)S(1)}, bf16[256,256]{1,0:T(8,128)(2,1)}, u32[]{:S(2)}) copy-start(bf16[256,256]{1,0:T(8,128)(2,1)} %param.17) | copy-start | bytes 393220
  0.7 11.9 %all-to-all-start = ((bf16[2,512,256]{2,1,0:T(8,128)(2,1)}), bf16[2,512,256]{2,1,0:T(8,128)(2,1)S(1)}, u32[]{:S(2)}, u32[]{:S(2)}) async-start(bf16[2,512,256]{2,1,0:T(8,128)(2,1)} %bitcast.117), calls=%async_computation | async-start | bytes 1048576 | tf_op jit(solution)/shard_map/all_to_all | solution.py:15
  13.2 17.4 %all-to-all-start.1 = ((bf16[32,16,256]{2,1,0:T(8,128)(2,1)}), bf16[32,16,256]{2,1,0:T(8,128)(2,1)S(1)}, u32[]{:S(2)}, u32[]{:S(2)}) async-start(bf16[32,16,256]{2,1,0:T(8,128)(2,1)} %bitcast.11), calls=%async_computation.1 | async-start | bytes 524288 | tf_op jit(solution)/shard_map/all_to_all | solution.py:18
  31.4 16.5 %all-to-all-start.2 = ((bf16[32,16,256]{2,1,0:T(8,128)(2,1)}), bf16[32,16,256]{2,1,0:T(8,128)(2,1)S(1)}, u32[]{:S(2)}, u32[]{:S(2)}) async-start(bf16[32,16,256]{2,1,0:T(8,128)(2,1)} %broadcast_in_dim.55), calls=%async_computation.2 | async-start | bytes 524288 | tf_op jit(solution)/shard_map/all_to_all | solution.py:26
  68.4 1.1 copy-start
  69.6 25.3 %collective-permute-start = (f32[512,256]{1,0:T(8,128)S(1)}, f32[512,256]{1,0:T(8,128)S(1)}, u32[]{:S(2)}, u32[]{:S(2)}) collective-permute-start(f32[512,256]{1,0:T(8,128)S(1)} %dynamic-slice_bitcast_fusion), channel_id=1, source_target_pairs={{0,8},{8,0},{1,9},{9,1},{2,10},{10,2},{3,11},{11,3},{4,12},{12,4},... | collective-permute-start | bytes 1572872 | tf_op jit(solution)/shard_map/ppermute | solution.py:37
  85.1 19.3 %all-to-all-start.4 = ((bf16[8,32,256]{2,1,0:T(8,128)(2,1)}), bf16[8,32,256]{2,1,0:T(8,128)(2,1)S(1)}, u32[]{:S(2)}, u32[]{:S(2)}) async-start(bf16[8,32,256]{2,1,0:T(8,128)(2,1)} %bitcast.22), calls=%async_computation.4 | async-start | bytes 262144 | tf_op jit(solution)/shard_map/all_to_all | solution.py:126
  104.5 15.6 %all-to-all-start.5 = ((bf16[32,16,256]{2,1,0:T(8,128)(2,1)}), bf16[32,16,256]{2,1,0:T(8,128)(2,1)S(1)}, u32[]{:S(2)}, u32[]{:S(2)}) async-start(bf16[32,16,256]{2,1,0:T(8,128)(2,1)} %bitcast.27), calls=%async_computation.5 | async-start | bytes 524288 | tf_op jit(solution)/shard_map/all_to_all | solution.py:39
  120.0 15.0 %all-to-all-start.3 = ((bf16[8,32,1024]{2,1,0:T(8,128)(2,1)}), bf16[8,32,1024]{2,1,0:T(8,128)(2,1)S(1)}, u32[]{:S(2)}, u32[]{:S(2)}) async-start(bf16[8,32,1024]{2,1,0:T(8,128)(2,1)} %bitcast.20), calls=%async_computation.3 | async-start | bytes 1048576 | tf_op jit(solution)/shard_map/all_to_all | solution.py:125
  135.7 24.1 %all-to-all-start.6 = ((bf16[32,16,256]{2,1,0:T(8,128)(2,1)}), bf16[32,16,256]{2,1,0:T(8,128)(2,1)S(1)}, u32[]{:S(2)}, u32[]{:S(2)}) async-start(bf16[32,16,256]{2,1,0:T(8,128)(2,1)} %broadcast_in_dim.56), calls=%async_computation.6 | async-start | bytes 524288 | tf_op jit(solution)/shard_map/all_to_all | solution.py:26

commit v2 on v1

v2 whole, which is shorter than its diff:
```python
import math

import jax
import jax.numpy as jnp
from jax import lax
from jax.experimental import pallas as pl
from jax.experimental.pallas import tpu as pltpu
from jax.sharding import PartitionSpec as P

NT = (((1,), (1,)), ((), ()))
LOG2E = 1.4426950408889634


def dot(a, b, dims=(((1,), (0,)), ((), ()))):
    return lax.dot_general(a, b, dims, preferred_element_type=jnp.float32)


def attention_kernel(
    core_ref, length_ref, query_ref, grad_ref, prompt_ref, cont_ref,
    own_ref, other_ref, token_ref, key_ref, value_ref, turned_ref, dk_ref, dv_ref
):
    tokens, width = query_ref.shape
    prompt_len = prompt_ref.shape[0]
    hd = cont_ref.shape[1] // 2
    heads = width // hd
    peers, share, _ = token_ref.shape
    scale = 1.0 / math.sqrt(hd)
    key_ref[:prompt_len] = prompt_ref[:, :hd]
    key_ref[prompt_len:] = cont_ref[:, :hd]
    value_ref[:prompt_len] = prompt_ref[:, hd:]
    value_ref[prompt_len:] = cont_ref[:, hd:]
    turned_ref[...] = key_ref[...].astype(jnp.float32).T.astype(jnp.bfloat16)
    length = length_ref[0]
    live = lax.broadcasted_iota(jnp.int32, (tokens, hd), 0) < length
    causal = lax.broadcasted_iota(jnp.int32, (tokens, tokens), 0) <= lax.broadcasted_iota(
        jnp.int32, (tokens, tokens), 1
    )
    for head in range(heads):
        cols = slice(head * hd, (head + 1) * hd)
        q = query_ref[:, cols]
        g = jnp.where(live, grad_ref[:, cols], jnp.zeros((), jnp.bfloat16))
        s = dot(key_ref[...], q, NT)
        s = jnp.concatenate(
            [s[:prompt_len], jnp.where(causal, s[prompt_len:], -1e30)], 0
        )
        top = jnp.max(s, axis=0, keepdims=True) * (scale * LOG2E)
        e = jnp.exp2(s * (scale * LOG2E) - top)
        inv = 1.0 / jnp.sum(e, axis=0, keepdims=True)
        d = dot(value_ref[...], g, NT)
        delta = jnp.sum(e * d, axis=0, keepdims=True) * inv
        probs = e * inv
        w = probs.astype(jnp.bfloat16)
        ds = (probs * (d - delta) * scale).astype(jnp.bfloat16)
        dk = dot(ds, q)
        dv = dot(w, g)
        if head == 0:
            dk_ref[...] = dk
            dv_ref[...] = dv
        else:
            dk_ref[...] += dk
            dv_ref[...] += dv
        dq = dot(turned_ref[...], ds).T.astype(jnp.bfloat16)
        token_ref[:, :, cols] = dq.reshape(peers, share, hd)
    half = prompt_len // 2
    core = core_ref[0]
    mine = pl.ds(pl.multiple_of(core * half, half), half)
    theirs = pl.ds(pl.multiple_of((1 - core) * half, half), half)
    own_ref[:, :hd] = dk_ref[mine]
    own_ref[:, hd:] = dv_ref[mine]
    other_ref[:, :hd] = dk_ref[theirs]
    other_ref[:, hd:] = dv_ref[theirs]
    token_ref[:, :, width : width + hd] = (
        dk_ref[prompt_len:].astype(jnp.bfloat16).reshape(peers, share, hd)
    )
    token_ref[:, :, width + hd :] = (
        dv_ref[prompt_len:].astype(jnp.bfloat16).reshape(peers, share, hd)
    )


def attention_grads(query, grad, prompt, cont, core, length, peers):
    tokens, width = query.shape
    prompt_len, both = prompt.shape
    hd = both // 2
    keys = prompt_len + tokens
    return pl.pallas_call(
        attention_kernel,
        out_shape=(
            jax.ShapeDtypeStruct((prompt_len // 2, both), jnp.float32),
            jax.ShapeDtypeStruct((prompt_len // 2, both), jnp.float32),
            jax.ShapeDtypeStruct((peers, tokens // peers, width + both), jnp.bfloat16),
        ),
        in_specs=[pl.BlockSpec(memory_space=pltpu.SMEM)] * 2
        + [pl.BlockSpec(memory_space=pltpu.VMEM)] * 4,
        out_specs=[pl.BlockSpec(memory_space=pltpu.VMEM)] * 3,
        scratch_shapes=[
            pltpu.VMEM((keys, hd), jnp.bfloat16),
            pltpu.VMEM((keys, hd), jnp.bfloat16),
            pltpu.VMEM((hd, keys), jnp.bfloat16),
            pltpu.VMEM((keys, hd), jnp.float32),
            pltpu.VMEM((keys, hd), jnp.float32),
        ],
        compiler_params=pltpu.CompilerParams(vmem_limit_bytes=48 * 2**20),
    )(core, length, query, grad, prompt, cont)


CHIPS = ("zl", "y")
GROUP = ("zl", "y", "core")
SWAP = [(0, 1), (1, 0)]


def spread(block, root):
    rows, width = block.shape
    peers = lax.axis_size(CHIPS)
    halves = lax.all_to_all(block.reshape(2, rows // 2, width), "core", 0, 0, tiled=True)
    half = lax.dynamic_index_in_dim(halves, root % 2, 0, keepdims=False)
    pieces = half.reshape(peers, rows // 2 // peers, width)
    pieces = lax.all_to_all(pieces, CHIPS, 0, 0, tiled=True)
    piece = lax.dynamic_index_in_dim(pieces, root // 2, 0, keepdims=True)
    return collect(piece, rows, width)


def collect(piece, rows, width):
    peers = lax.axis_size(CHIPS)
    copies = jnp.broadcast_to(piece, (peers, *piece.shape[1:]))
    half = lax.all_to_all(copies, CHIPS, 0, 0, tiled=True).reshape(rows // 2, width)
    return lax.all_gather(half, "core", tiled=True)


def total_over_group(own, other):
    rows, width = own.shape
    peers = lax.axis_size(CHIPS)
    half = own + lax.ppermute(other, "core", SWAP)
    pieces = half.astype(jnp.bfloat16).reshape(peers, rows // peers, width)
    pieces = lax.all_to_all(pieces, CHIPS, 0, 0, tiled=True)
    piece = jnp.sum(pieces.astype(jnp.float32), axis=0, keepdims=True).astype(jnp.bfloat16)
    return collect(piece, 2 * rows, width)


def body(query, cont_kv, prompt_kv, out_grad, lengths, owners):
    root = owners[0]
    width = query.shape[1]
    core = lax.axis_index("core").astype(jnp.int32)[None]
    heads = lax.axis_size("kv")
    shared = spread(prompt_kv[0], root)
    own, other, token = attention_grads(
        query, out_grad, shared, cont_kv, core, lengths, heads
    )
    token = lax.all_to_all(token, "kv", 0, 0, tiled=True)
    token = token.transpose(1, 0, 2)
    token_query = token[:, :, :width].reshape(-1, heads * width)
    token_cont = token[:, :, width:].reshape(-1, heads * cont_kv.shape[1])
    total = total_over_group(own, other)
    mine = lax.axis_index(GROUP) == root
    grad_prompt = jnp.where(mine, total, jnp.zeros((), jnp.bfloat16))
    return (token_query, token_cont, grad_prompt[None])


def solution(mesh):
    fine = jax.sharding.Mesh(mesh.devices.reshape(4, 8, 2, 8), (*GROUP, "kv"))
    placed = (
        P(GROUP, "kv"),
        P(GROUP, "kv"),
        P(GROUP, None, "kv"),
        P(GROUP, "kv"),
        P(GROUP),
        P("kv"),
    )
    return jax.shard_map(
        body,
        mesh=fine,
        in_specs=placed,
        out_specs=(P((*GROUP, "kv"), None), P((*GROUP, "kv"), None), P(GROUP, None, "kv")),
        check_vma=False,
    )
```

time: 166 us -> 138 us (0.83)
  starting transfers between devices: 70.7 us -> 51.5 us
  blocking collectives: 9.84 us -> 24.7 us
  waiting for transfers between devices: 55.6 us -> 42.3 us
  Pallas kernels: 0 us -> 12.2 us
  local copies, waits for them, and re-layouts: 12.1 us -> 3.74 us
  matrix products: 7.46 us -> 0 us
  other arithmetic: 7.16 us -> 0.95 us
    all_to_all x3 -> x1, waiting for transfers between devices: 28.5 us -> 12.3 us  [body(): token = lax.all_to_all(token, 'kv', 0, 0, tiled=True)]
    all_to_all x0 -> x1, blocking collectives: none -> 13.7 us  [total_over_group(): pieces = lax.all_to_all(pieces, CHIPS, 0, 0, tiled=True)]
    pallas_call x0 -> x1, Pallas kernels: none -> 12.2 us  [attention_grads(): pl.pallas_call(attention_kernel, out_shape=(jax.ShapeDtypeStruct((prompt_...]
    ppermute x1, starting transfers between devices: 13.9 us -> 2.27 us  [total_over_group(): half = own + lax.ppermute(other, 'core', SWAP)]
    all_to_all x3 -> x1, starting transfers between devices: 18.8 us -> 9.77 us  [body(): token = lax.all_to_all(token, 'kv', 0, 0, tiled=True)]
    dot_general x6 -> x0, matrix products: 7.46 us -> none  [the longest x1 2.42 us: window_grads(): lax.dot_general(q_rows, keys, (((1,), (1,)), ((), ())), preferred_element...]
    slice x6 -> x0, local copies, waits for them, and re-layouts: 2.84 us -> none  [the longest x1 1.62 us: body(): grad_cont = total[prompt_len:].astype(jnp.bfloat16)]
    concatenate x3 -> x0, other arithmetic: 2.63 us -> none  [the longest x1 1.78 us: body(): grad_query = jnp.concatenate(grad_blocks, 0)]
  transfers between devices with their start and end apart: 8 -> 6, of which waited for: 7 -> 6; matrix products, arithmetic and copies ran while one was open for 5% -> 1% of each run, Pallas kernels for 0% -> 0%
where the time goes in v2:
time: 138 us
  starting transfers between devices  51.5 us (37%)
  waiting for transfers between devices  42.3 us (31%)
  blocking collectives  24.7 us (18%)
  Pallas kernels  12.2 us (9%)
  local copies, waits for them, and re-layouts  3.74 us (3%)
  between operations  2.13 us (2%)
    all_to_all x2, starting transfers between devices, collect(): lax.all_to_all(copies, CHIPS, 0, 0, tiled=True).reshape(rows // 2, width)  21.9 us
    all_to_all x2, waiting for transfers between devices, collect(): lax.all_to_all(copies, CHIPS, 0, 0, tiled=True).reshape(rows // 2, width)  17.6 us
    all_to_all x1, blocking collectives, total_over_group(): pieces = lax.all_to_all(pieces, CHIPS, 0, 0, tiled=True)  13.7 us
    all_to_all x1, waiting for transfers between devices, body(): token = lax.all_to_all(token, 'kv', 0, 0, tiled=True)  12.3 us
    pallas_call x1, Pallas kernels, attention_grads(): pl.pallas_call(attention_kernel, out_shape=(jax.ShapeDtypeStruct((prompt_...  12.2 us
    all_gather x2, blocking collectives, collect(): return lax.all_gather(half, 'core', tiled=True)  11 us
    all_to_all x1, starting transfers between devices, spread(): lax.all_to_all(block.reshape(2, rows // 2, width), 'core', 0, 0, tiled=True)  10.4 us
    all_to_all x1, waiting for transfers between devices, spread(): pieces = lax.all_to_all(pieces, CHIPS, 0, 0, tiled=True)  10.1 us
  transfers between devices with their start and end apart: 6, of which 6 were waited for; matrix products, arithmetic and copies ran while one was open for 1% of the time, Pallas kernels for 0%

profile of v2, /device:TPU:1, one launch (start us, length us, event | category | flops | bytes accessed | tf_op | source)
XLA Modules:
  0.0 137.5 jit_solution(16291609769206002486)
XLA Ops:
  0.6 10.4 %all-to-all-start = ((bf16[2,512,256]{2,1,0:T(8,128)(2,1)}), bf16[2,512,256]{2,1,0:T(8,128)(2,1)S(1)}, u32[]{:S(2)}, u32[]{:S(2)}) async-start(bf16[2,512,256]{2,1,0:T(8,128)(2,1)} %bitcast.28), calls=%async_computation | async-start | bytes 1048576 | tf_op jit(solution)/shard_map/all_to_all | solution.py:114
  11.7 0.7 all-to-all-done
  12.4 0.7 constant_dynamic-slice_fusion
  13.1 7.3 %all-to-all-start.1 = ((bf16[32,16,256]{2,1,0:T(8,128)(2,1)}), bf16[32,16,256]{2,1,0:T(8,128)(2,1)S(1)}, u32[]{:S(2)}, u32[]{:S(2)}) async-start(bf16[32,16,256]{2,1,0:T(8,128)(2,1)} %bitcast.3), calls=%async_computation.1 | async-start | bytes 524288 | tf_op jit(solution)/shard_map/all_to_all | solution.py:117
  20.4 10.1 %all-to-all-done.1 = bf16[32,16,256]{2,1,0:T(8,128)(2,1)S(1)} async-done(((bf16[32,16,256]{2,1,0:T(8,128)(2,1)}), bf16[32,16,256]{2,1,0:T(8,128)(2,1)S(1)}, u32[]{:S(2)}, u32[]{:S(2)}) %all-to-all-start.1) | async-done | bytes 262176 | tf_op jit(solution)/shard_map/all_to_all | solution.py:117
  30.5 0.7 broadcast_in_dim.25
  31.2 0.0 copy-start.1
  31.2 6.5 %all-to-all-start.2 = ((bf16[32,16,256]{2,1,0:T(8,128)(2,1)}), bf16[32,16,256]{2,1,0:T(8,128)(2,1)S(1)}, u32[]{:S(2)}, u32[]{:S(2)}) async-start(bf16[32,16,256]{2,1,0:T(8,128)(2,1)} %broadcast_in_dim.25), calls=%async_computation.2 | async-start | bytes 524288 | tf_op jit(solution)/shard_map/all_to_all | solution.py:125
  37.8 0.0 copy-start
  38.5 9.4 %all-to-all-done.2 = bf16[32,16,256]{2,1,0:T(8,128)(2,1)S(1)} async-done(((bf16[32,16,256]{2,1,0:T(8,128)(2,1)}), bf16[32,16,256]{2,1,0:T(8,128)(2,1)S(1)}, u32[]{:S(2)}, u32[]{:S(2)}) %all-to-all-start.2) | async-done | bytes 262176 | tf_op jit(solution)/shard_map/all_to_all | solution.py:125
  47.9 0.0 copy-start.2
  47.9 5.3 %all_gather.6.prompt_ref = bf16[1024,256]{1,0:T(8,128)(2,1)S(1)} all-gather(bf16[512,256]{1,0:T(8,128)(2,1)S(1)} %bitcast.26), channel_id=1, replica_groups=mesh['zl'=4,'y'=8,'core'=2,'kv'=8] {'core'}, dimensions={0}, use_global_device_ids=true | all-gather | bytes 786432 | tf_op jit(solution)/shard_map/all_gather | solution.py:126
  53.2 0.0 copy-done.1
  53.2 0.0 copy-done
  53.2 0.0 copy-done.2
  53.2 12.2 %shard_map.85 = (f32[512,256]{1,0:T(8,128)S(1)}, f32[512,256]{1,0:T(8,128)S(1)}, bf16[8,32,1280]{2,1,0:T(8,128)(2,1)}) custom-call(s32[1]{0:T(128)} %bitcast.core_ref, s32[1]{0:T(128)S(6)} %copy.13.length_ref, bf16[256,1024]{1,0:T(8,128)(2,1)S(1)} %copy-done, bf16[256,1024]{1,0:T(8,128)(2,1)S(1)} %copy-done.1, bf16[1024,256]{1,0:T(8,128)(2,1)S(1)} %all_gather.6.prompt_ref, ...), custom_call_target="tpu_custom_call" | custom-call | tf_op jit(solution)/shard_map/pallas_call | solution.py:85
  65.4 2.3 %collective-permute-start = (f32[512,256]{1,0:T(8,128)S(1)}, f32[512,256]{1,0:T(8,128)S(1)}, u32[]{:S(2)}, u32[]{:S(2)}) collective-permute-start(f32[512,256]{1,0:T(8,128)S(1)} %get-tuple-element.8), channel_id=1, source_target_pairs={{0,8},{8,0},{1,9},{9,1},{2,10},{10,2},{3,11},{11,3},{4,12},{12,4},... | collective-permute-start | bytes 1572872 | tf_op jit(solution)/shard_map/ppermute | solution.py:132
  67.6 1.5 %collective-permute-done = f32[512,256]{1,0:T(8,128)S(1)} collective-permute-done((f32[512,256]{1,0:T(8,128)S(1)}, f32[512,256]{1,0:T(8,128)S(1)}, u32[]{:S(2)}, u32[]{:S(2)}) %collective-permute-start) | collective-permute-done | bytes 524320 | tf_op jit(solution)/shard_map/ppermute | solution.py:132
  69.1 0.1 add_convert_fusion
  69.2 13.7 %all_to_all.30 = bf16[32,16,256]{2,1,0:T(8,128)(2,1)S(1)} all-to-all(bf16[32,16,256]{2,1,0:T(8,128)(2,1)S(1)} %bitcast.27), channel_id=1, replica_groups=mesh['zl'=4,'y'=8,'core'=2,'kv'=8] {'zl','y'}, dimensions={0} | all-to-all | bytes 524288 | tf_op jit(solution)/shard_map/all_to_all | solution.py:134
  82.9 9.8 %all-to-all-start.3 = ((bf16[8,32,1280]{2,1,0:T(8,128)(2,1)}), bf16[8,32,1280]{2,1,0:T(8,128)(2,1)S(1)}, u32[]{:S(2)}, u32[]{:S(2)}) async-start(bf16[8,32,1280]{2,1,0:T(8,128)(2,1)} %get-tuple-element.6), calls=%async_computation.3 | async-start | bytes 1310720 | tf_op jit(solution)/shard_map/all_to_all | solution.py:148
  92.7 0.1 reduce_sum.12
  92.8 12.3 %all-to-all-done.3 = bf16[8,32,1280]{2,1,0:T(8,128)(2,1)S(1)} async-done(((bf16[8,32,1280]{2,1,0:T(8,128)(2,1)}), bf16[8,32,1280]{2,1,0:T(8,128)(2,1)S(1)}, u32[]{:S(2)}, u32[]{:S(2)}) %all-to-all-start.3) | async-done | bytes 655392 | tf_op jit(solution)/shard_map/all_to_all | solution.py:148
  105.0 0.7 broadcast_in_dim.26
  105.8 15.4 %all-to-all-start.5 = ((bf16[32,16,256]{2,1,0:T(8,128)(2,1)}), bf16[32,16,256]{2,1,0:T(8,128)(2,1)S(1)}, u32[]{:S(2)}, u32[]{:S(2)}) async-start(bf16[32,16,256]{2,1,0:T(8,128)(2,1)} %broadcast_in_dim.26), calls=%async_computation.5 | async-start | bytes 524288 | tf_op jit(solution)/shard_map/all_to_all | solution.py:125
  121.2 0.1 slice_bitcast_fusion
  121.2 0.8 copy.11
  122.1 0.7 copy.12
  122.7 8.3 %all-to-all-done.5 = bf16[32,16,256]{2,1,0:T(8,128)(2,1)S(1)} async-done(((bf16[32,16,256]{2,1,0:T(8,128)(2,1)}), bf16[32,16,256]{2,1,0:T(8,128)(2,1)S(1)}, u32[]{:S(2)}, u32[]{:S(2)}) %all-to-all-start.5) | async-done | bytes 262176 | tf_op jit(solution)/shard_map/all_to_all | solution.py:125
  131.0 5.7 %all_gather.7 = bf16[1024,256]{1,0:T(8,128)(2,1)S(1)} all-gather(bf16[512,256]{1,0:T(8,128)(2,1)S(1)} %bitcast.25), channel_id=1, replica_groups=mesh['zl'=4,'y'=8,'core'=2,'kv'=8] {'core'}, dimensions={0}, use_global_device_ids=true | all-gather | bytes 786432 | tf_op jit(solution)/shard_map/all_gather | solution.py:126
  136.7 0.8 select_bitcast_fusion
  (2 shorter events, 0.0 us)
Async XLA Ops:
  0.6 11.7 %all-to-all-start = ((bf16[2,512,256]{2,1,0:T(8,128)(2,1)}), bf16[2,512,256]{2,1,0:T(8,128)(2,1)S(1)}, u32[]{:S(2)}, u32[]{:S(2)}) async-start(bf16[2,512,256]{2,1,0:T(8,128)(2,1)} %bitcast.28), calls=%async_computation | async-start | bytes 1048576 | tf_op jit(solution)/shard_map/all_to_all | solution.py:114
  13.1 17.4 %all-to-all-start.1 = ((bf16[32,16,256]{2,1,0:T(8,128)(2,1)}), bf16[32,16,256]{2,1,0:T(8,128)(2,1)S(1)}, u32[]{:S(2)}, u32[]{:S(2)}) async-start(bf16[32,16,256]{2,1,0:T(8,128)(2,1)} %bitcast.3), calls=%async_computation.1 | async-start | bytes 524288 | tf_op jit(solution)/shard_map/all_to_all | solution.py:117
  31.2 21.9 %copy-start.1 = (bf16[256,1024]{1,0:T(8,128)(2,1)S(1)}, bf16[256,1024]{1,0:T(8,128)(2,1)}, u32[]{:S(2)}) copy-start(bf16[256,1024]{1,0:T(8,128)(2,1)} %grad_ref.1) | copy-start | bytes 1572868
  31.2 16.6 %all-to-all-start.2 = ((bf16[32,16,256]{2,1,0:T(8,128)(2,1)}), bf16[32,16,256]{2,1,0:T(8,128)(2,1)S(1)}, u32[]{:S(2)}, u32[]{:S(2)}) async-start(bf16[32,16,256]{2,1,0:T(8,128)(2,1)} %broadcast_in_dim.25), calls=%async_computation.2 | async-start | bytes 524288 | tf_op jit(solution)/shard_map/all_to_all | solution.py:125
  37.8 15.4 %copy-start = (bf16[256,1024]{1,0:T(8,128)(2,1)S(1)}, bf16[256,1024]{1,0:T(8,128)(2,1)}, u32[]{:S(2)}) copy-start(bf16[256,1024]{1,0:T(8,128)(2,1)} %query_ref.1) | copy-start | bytes 1572868
  47.9 5.3 %copy-start.2 = (bf16[256,256]{1,0:T(8,128)(2,1)S(1)}, bf16[256,256]{1,0:T(8,128)(2,1)}, u32[]{:S(2)}) copy-start(bf16[256,256]{1,0:T(8,128)(2,1)} %cont_ref.1) | copy-start | bytes 393220
  65.4 3.8 %collective-permute-start = (f32[512,256]{1,0:T(8,128)S(1)}, f32[512,256]{1,0:T(8,128)S(1)}, u32[]{:S(2)}, u32[]{:S(2)}) collective-permute-start(f32[512,256]{1,0:T(8,128)S(1)} %get-tuple-element.8), channel_id=1, source_target_pairs={{0,8},{8,0},{1,9},{9,1},{2,10},{10,2},{3,11},{11,3},{4,12},{12,4},... | collective-permute-start | bytes 1572872 | tf_op jit(solution)/shard_map/ppermute | solution.py:132
  82.9 22.1 %all-to-all-start.3 = ((bf16[8,32,1280]{2,1,0:T(8,128)(2,1)}), bf16[8,32,1280]{2,1,0:T(8,128)(2,1)S(1)}, u32[]{:S(2)}, u32[]{:S(2)}) async-start(bf16[8,32,1280]{2,1,0:T(8,128)(2,1)} %get-tuple-element.6), calls=%async_computation.3 | async-start | bytes 1310720 | tf_op jit(solution)/shard_map/all_to_all | solution.py:148
  105.8 25.2 %all-to-all-start.5 = ((bf16[32,16,256]{2,1,0:T(8,128)(2,1)}), bf16[32,16,256]{2,1,0:T(8,128)(2,1)S(1)}, u32[]{:S(2)}, u32[]{:S(2)}) async-start(bf16[32,16,256]{2,1,0:T(8,128)(2,1)} %broadcast_in_dim.26), calls=%async_computation.5 | async-start | bytes 524288 | tf_op jit(solution)/shard_map/all_to_all | solution.py:125

commit v3 on v2

v3 whole, which is shorter than its diff:
```python
import math

import jax
import jax.numpy as jnp
from jax import lax
from jax.experimental import pallas as pl
from jax.experimental.pallas import tpu as pltpu
from jax.sharding import PartitionSpec as P

NT = (((1,), (1,)), ((), ()))
LOG2E = 1.4426950408889634
CHIPS = ("zl", "y")
GROUP = ("zl", "y", "core")
OWNER, LENGTH, CORE, KV, MINE = range(5)
VMEM = pl.BlockSpec(memory_space=pltpu.VMEM)
SMEM = pl.BlockSpec(memory_space=pltpu.SMEM)
ANY = pl.BlockSpec(memory_space=pl.ANY)


def like(shape, dtype=jnp.bfloat16):
    return jax.ShapeDtypeStruct(shape, dtype)


def dot(a, b, dims=(((1,), (0,)), ((), ()))):
    return lax.dot_general(a, b, dims, preferred_element_type=jnp.float32)


def attention_kernel(
    facts_ref, query_ref, grad_ref, prompt_ref, cont_ref, own_ref, other_ref, keep_ref,
    give_ref, key_ref, value_ref, turned_ref, dk_ref, dv_ref
):
    tokens, width = query_ref.shape
    prompt_len = prompt_ref.shape[0]
    hd = cont_ref.shape[1] // 2
    heads = width // hd
    ring, share, _ = keep_ref.shape
    around, side = facts_ref[KV] // 2, facts_ref[KV] % 2
    scale = 1.0 / math.sqrt(hd)
    key_ref[:prompt_len] = prompt_ref[:, :hd]
    key_ref[prompt_len:] = cont_ref[:, :hd]
    value_ref[:prompt_len] = prompt_ref[:, hd:]
    value_ref[prompt_len:] = cont_ref[:, hd:]
    turned_ref[...] = key_ref[...].astype(jnp.float32).T.astype(jnp.bfloat16)
    live = lax.broadcasted_iota(jnp.int32, (tokens, hd), 0) < facts_ref[LENGTH]
    causal = lax.broadcasted_iota(jnp.int32, (tokens, tokens), 0) <= lax.broadcasted_iota(
        jnp.int32, (tokens, tokens), 1
    )

    def hand_out(grads, columns):
        blocks = grads.reshape(ring, 2, share, hd)
        same = jnp.full((share, hd), side, jnp.int32) == 0
        for x in range(ring):
            distance = (x - around + ring) % ring
            low, high = blocks[x, 0], blocks[x, 1]
            keep_ref[distance, :, columns] = jnp.where(same, low, high)
            give_ref[distance, :, columns] = jnp.where(same, high, low)

    def products(head):
        cols = slice(head * hd, (head + 1) * hd)
        q = query_ref[:, cols]
        g = jnp.where(live, grad_ref[:, cols], jnp.zeros((), jnp.bfloat16))
        s = dot(key_ref[...], q, NT)
        s = jnp.concatenate([s[:prompt_len], jnp.where(causal, s[prompt_len:], -1e30)], 0)
        return q, g, s, dot(value_ref[...], g, NT)

    ahead = products(0)
    for head in range(heads):
        q, g, s, d = ahead
        if head + 1 < heads:
            ahead = products(head + 1)
        top = jnp.max(s, axis=0, keepdims=True) * (scale * LOG2E)
        e = jnp.exp2(s * (scale * LOG2E) - top)
        inv = 1.0 / jnp.sum(e, axis=0, keepdims=True)
        delta = jnp.sum(e * d, axis=0, keepdims=True) * inv
        probs = e * inv
        w = probs.astype(jnp.bfloat16)
        ds = (probs * (d - delta) * scale).astype(jnp.bfloat16)
        dk = dot(ds, q)
        dv = dot(w, g)
        if head == 0:
            dk_ref[...] = dk
            dv_ref[...] = dv
        else:
            dk_ref[...] += dk
            dv_ref[...] += dv
        dq = dot(turned_ref[...], ds).T.astype(jnp.bfloat16)
        hand_out(dq, slice(head * hd, (head + 1) * hd))
    half = prompt_len // 2
    mine = pl.ds(pl.multiple_of(facts_ref[CORE] * half, half), half)
    theirs = pl.ds(pl.multiple_of((1 - facts_ref[CORE]) * half, half), half)
    for ref, first in ((dk_ref, 0), (dv_ref, hd)):
        own_ref[:, first : first + hd] = ref[mine]
        other_ref[:, first : first + hd] = ref[theirs].astype(jnp.bfloat16)
        hand_out(
            ref[prompt_len:].astype(jnp.bfloat16), slice(width + first, width + first + hd)
        )


def attention_grads(query, grad, prompt, cont, facts, ring):
    tokens, width = query.shape
    prompt_len, both = prompt.shape
    hd = both // 2
    keys = prompt_len + tokens
    blocks = like((ring, tokens // ring // 2, width + both))
    return pl.pallas_call(
        attention_kernel,
        out_shape=(
            like((prompt_len // 2, both), jnp.float32),
            like((prompt_len // 2, both)),
            blocks,
            blocks,
        ),
        in_specs=[SMEM] + [VMEM] * 4,
        out_specs=[VMEM] * 4,
        scratch_shapes=[
            pltpu.VMEM((keys, hd), jnp.bfloat16),
            pltpu.VMEM((keys, hd), jnp.bfloat16),
            pltpu.VMEM((hd, keys), jnp.bfloat16),
            pltpu.VMEM((keys, hd), jnp.float32),
            pltpu.VMEM((keys, hd), jnp.float32),
        ],
        compiler_params=pltpu.CompilerParams(vmem_limit_bytes=48 * 2**20),
    )(facts, query, grad, prompt, cont)


def local_call(kernel, outs, *arrays, scratch=(), places=None):
    return pl.pallas_call(
        kernel,
        out_shape=outs,
        in_specs=places or [VMEM] * len(arrays),
        out_specs=jax.tree.map(lambda _: VMEM, outs),
        scratch_shapes=scratch,
        compiler_params=pltpu.CompilerParams(vmem_limit_bytes=8 * 2**20),
    )(*arrays)


def pick_half(facts_ref, own_ref, other_ref, half_ref, sem):
    core, half = facts_ref[CORE], half_ref.shape[0]
    rows = pl.ds(pl.multiple_of(core * half, half), half)
    here = facts_ref[OWNER] % 2 == core

    @pl.when(here)
    def _():
        copy = pltpu.make_async_copy(own_ref.at[rows], half_ref, sem)
        copy.start()
        copy.wait()

    @pl.when(jnp.logical_not(here))
    def _():
        half_ref[...] = other_ref[rows]


def pick_piece(facts_ref, pieces_ref, copies_ref):
    piece = pieces_ref[facts_ref[OWNER] // 2]
    for peer in range(copies_ref.shape[0]):
        copies_ref[peer] = piece


def add_halves(own_ref, other_ref, pieces_ref):
    half = own_ref[...] + other_ref[...].astype(jnp.float32)
    pieces_ref[...] = half.astype(jnp.bfloat16).reshape(pieces_ref.shape)


def sum_pieces(pieces_ref, keep_ref, got_ref, copies_ref, *sends):
    for distance, send in enumerate(sends):
        send[0] = keep_ref[distance + 1]
        send[1] = got_ref[distance + 1]
    piece = jnp.sum(pieces_ref[...].astype(jnp.float32), axis=0).astype(jnp.bfloat16)
    for peer in range(copies_ref.shape[0]):
        copies_ref[peer] = piece


def finish(facts_ref, total_ref, keep_ref, got_ref, *rest):
    came, (query_ref, cont_ref, prompt_ref) = rest[:-3], rest[-3:]
    ring, _, width = keep_ref.shape
    cont = cont_ref.shape[1] // (2 * ring)
    size = width - cont
    around, side = facts_ref[KV] // 2, facts_ref[KV] % 2
    for distance in range(ring):
        for slot in range(2):
            if distance:
                block = came[distance - 1].at[slot]
            else:
                block = (keep_ref, got_ref)[slot].at[0]
            head = (around - distance + ring) % ring * 2 + (side if slot == 0 else 1 - side)
            for ref, first, count in ((query_ref, 0, size), (cont_ref, size, cont)):
                columns = pl.ds(pl.multiple_of(head * count, count), count)
                ref[:, columns] = block[:, first : first + count]
    mine = facts_ref[MINE] == 1

    @pl.when(mine)
    def _():
        prompt_ref[0] = total_ref[...]

    @pl.when(jnp.logical_not(mine))
    def _():
        prompt_ref[...] = jnp.zeros_like(prompt_ref)


def collect(copies):
    half = lax.all_to_all(copies, CHIPS, 0, 0, tiled=True)
    return lax.all_gather(half.reshape(-1, half.shape[-1]), "core", tiled=True)


def swap(block, axis):
    pairs = [(i, i ^ 1) for i in range(lax.axis_size(axis))]
    return lax.ppermute(block, axis, pairs)


def body(query, cont_kv, prompt_kv, out_grad, lengths, owners):
    rows, both = prompt_kv.shape[1:]
    heads, chips = lax.axis_size("kv"), lax.axis_size(CHIPS)
    ring = heads // 2
    tokens, width = query.shape
    mine = lax.axis_index(GROUP) == owners[0]
    core, place = lax.axis_index("core"), lax.axis_index("kv")
    facts = [owners[0], lengths[0], core, place, mine]
    facts = jnp.stack([fact.astype(jnp.int32) for fact in facts])
    pieces = like((chips, rows // 2 // chips, both))

    other = swap(prompt_kv[0], "core")
    half = local_call(
        pick_half, like((rows // 2, both)), facts, prompt_kv[0], other,
        places=[SMEM, ANY, VMEM], scratch=[pltpu.SemaphoreType.DMA],
    )
    found = lax.all_to_all(half.reshape(pieces.shape), CHIPS, 0, 0, tiled=True)
    copies = local_call(pick_piece, pieces, facts, found, places=[SMEM, VMEM])
    shared = collect(copies)

    own, other, keep, give = attention_grads(query, out_grad, shared, cont_kv, facts, ring)
    other = swap(other, "core")
    got = swap(give, "kv")
    parts = local_call(add_halves, pieces, own, other)
    parts = lax.all_to_all(parts, CHIPS, 0, 0, tiled=True)
    send = like((2, *keep.shape[1:]))
    copies, *sends = local_call(sum_pieces, (pieces, *[send] * (ring - 1)), parts, keep, got)
    came = [
        lax.ppermute(block, "kv", [(i, (i + 2 * (n + 1)) % heads) for i in range(heads)])
        for n, block in enumerate(sends)
    ]
    total = collect(copies)
    outs = (
        like((tokens // heads, heads * width)),
        like((tokens // heads, heads * both)),
        like((1, rows, both)),
    )
    return local_call(
        finish, outs, facts, total, keep, got, *came, places=[SMEM] + [VMEM] * (ring + 2)
    )


def solution(mesh):
    fine = jax.sharding.Mesh(mesh.devices.reshape(4, 8, 2, 8), (*GROUP, "kv"))
    placed = (
        P(GROUP, "kv"),
        P(GROUP, "kv"),
        P(GROUP, None, "kv"),
        P(GROUP, "kv"),
        P(GROUP),
        P("kv"),
    )
    return jax.shard_map(
        body,
        mesh=fine,
        in_specs=placed,
        out_specs=(P((*GROUP, "kv"), None), P((*GROUP, "kv"), None), P(GROUP, None, "kv")),
        check_vma=False,
    )
```

time: 138 us -> 125 us (0.906)
  waiting for transfers between devices: 42.3 us -> 16 us
  blocking collectives: 24.7 us -> 43.3 us
  starting transfers between devices: 51.5 us -> 46.9 us
  local copies, waits for them, and re-layouts: 3.74 us -> 1.14 us
  Pallas kernels: 12.2 us -> 14.7 us
    all_to_all x5 -> x2, waiting for transfers between devices: 40.8 us -> 0.01 us  [the longest x1 0.01 us: body(): parts = lax.all_to_all(parts, CHIPS, 0, 0, tiled=True)]
    all_to_all x5 -> x2, starting transfers between devices: 49.3 us -> 17.3 us  [the longest x1 13.4 us: collect(): half = lax.all_to_all(copies, CHIPS, 0, 0, tiled=True)]
    ppermute x1 -> x6, starting transfers between devices: 2.27 us -> 29.6 us  [the longest x3 19 us: swap(): return lax.ppermute(block, axis, pairs)]
    all_to_all x1 -> x2, blocking collectives: 13.7 us -> 33.6 us  [the longest x1 17.2 us: body(): found = lax.all_to_all(half.reshape(pieces.shape), CHIPS, 0, 0, tiled=True)]
    ppermute x1 -> x6, waiting for transfers between devices: 1.52 us -> 16 us  [the longest x3 16 us: swap(): return lax.ppermute(block, axis, pairs)]
    pallas_call x1 -> x6, Pallas kernels: 12.2 us -> 14.7 us  [the longest x1 10.3 us: attention_grads(): pl.pallas_call(attention_kernel, out_shape=(like((prompt_len // 2, both),...]
    reshape x2 -> x0, local copies, waits for them, and re-layouts: 1.5 us -> none  [the longest x1 0.84 us: body(): token_query = token[:, :, :width].reshape(-1, heads * width)]
    broadcast_in_dim x3 -> x0, local copies, waits for them, and re-layouts: 1.44 us -> none  [collect(): copies = jnp.broadcast_to(piece, (peers, *piece.shape[1:]))]
  transfers between devices with their start and end apart: 6 -> 8, of which waited for: 6 -> 3; matrix products, arithmetic and copies ran while one was open for 1% -> 0% of each run, Pallas kernels for 0% -> 0%
where the time goes in v3:
time: 125 us; the launch traced here: 124 us
  starting transfers between devices  46.9 us (38%)
  blocking collectives  43.3 us (35%)
  waiting for transfers between devices  16 us (13%)
  Pallas kernels  14.7 us (12%)
  between operations  2.05 us (2%)
    ppermute x3, starting transfers between devices, swap(): return lax.ppermute(block, axis, pairs)  19 us
    all_to_all x1, blocking collectives, body(): found = lax.all_to_all(half.reshape(pieces.shape), CHIPS, 0, 0, tiled=True)  17.2 us
    all_to_all x1, blocking collectives, collect(): half = lax.all_to_all(copies, CHIPS, 0, 0, tiled=True)  16.4 us
    ppermute x3, waiting for transfers between devices, swap(): return lax.ppermute(block, axis, pairs)  16 us
    all_to_all x1, starting transfers between devices, collect(): half = lax.all_to_all(copies, CHIPS, 0, 0, tiled=True)  13.4 us
    ppermute x3, starting transfers between devices, body(): lax.ppermute(block, 'kv', [(i, (i + 2 * (n + 1)) % heads) for i in range(...  10.5 us
    pallas_call x1, Pallas kernels, attention_grads(): pl.pallas_call(attention_kernel, out_shape=(like((prompt_len // 2, both),...  10.3 us
    all_gather x2, blocking collectives, collect(): return lax.all_gather(half.reshape(-1, half.shape[-1]), 'core', tiled=True)  9.68 us
  transfers between devices with their start and end apart: 8, of which 3 were waited for; matrix products, arithmetic and copies ran while one was open for 0% of the time, Pallas kernels for 0%

profile of v3, /device:TPU:1, one launch (start us, length us, event | category | flops | bytes accessed | tf_op | source)
XLA Modules:
  0.0 124.0 jit_solution(17971160177387791239)
XLA Ops:
  0.6 8.8 %collective-permute-start = (bf16[1024,256]{1,0:T(8,128)(2,1)}, bf16[1024,256]{1,0:T(8,128)(2,1)S(1)}, u32[]{:S(2)}, u32[]{:S(2)}) collective-permute-start(bf16[1024,256]{1,0:T(8,128)(2,1)} %bitcast.10), channel_id=1, source_target_pairs={{0,8},{8,0},{1,9},{9,1},{2,10},{10,2},{3,11},{11,3},{4,12},{12,4},... | collective-permute-start | bytes 1572872 | tf_op jit(solution)/shard_map/ppermute | solution.py:207
  10.7 0.1 stack.19.facts_ref
  10.8 0.3 collective-permute-done.other_ref
  11.2 1.0 copy-done
  12.2 0.6 shard_map.85
  12.8 17.2 %all_to_all.20.pieces_ref = bf16[32,16,256]{2,1,0:T(8,128)(2,1)S(1)} all-to-all(bf16[32,16,256]{2,1,0:T(8,128)(2,1)S(1)} %bitcast.9), channel_id=1, replica_groups=mesh['zl'=4,'y'=8,'core'=2,'kv'=8] {'zl','y'}, dimensions={0} | all-to-all | bytes 524288 | tf_op jit(solution)/shard_map/all_to_all | solution.py:226
  30.0 0.6 shard_map.86
  30.6 0.0 copy-start.2
  30.6 16.4 %all_to_all.21 = bf16[32,16,256]{2,1,0:T(8,128)(2,1)S(1)} all-to-all(bf16[32,16,256]{2,1,0:T(8,128)(2,1)S(1)} %shard_map.86), channel_id=1, replica_groups=mesh['zl'=4,'y'=8,'core'=2,'kv'=8] {'zl','y'}, dimensions={0} | all-to-all | bytes 524288 | tf_op jit(solution)/shard_map/all_to_all | solution.py:201
  47.0 5.3 %all_gather.6.prompt_ref = bf16[1024,256]{1,0:T(8,128)(2,1)S(1)} all-gather(bf16[512,256]{1,0:T(8,128)(2,1)S(1)} %bitcast.13), channel_id=1, replica_groups=mesh['zl'=4,'y'=8,'core'=2,'kv'=8] {'core'}, dimensions={0}, use_global_device_ids=true | all-gather | bytes 786432 | tf_op jit(solution)/shard_map/all_gather | solution.py:202
  52.3 0.0 copy-done.2
  52.3 0.0 copy-done.1
  52.3 0.0 copy-done.3
  52.3 10.3 %shard_map.87 = (f32[512,256]{1,0:T(8,128)S(1)}, bf16[512,256]{1,0:T(8,128)(2,1)S(1)}, bf16[4,32,1280]{2,1,0:T(8,128)(2,1)S(1)}, bf16[4,32,1280]{2,1,0:T(8,128)(2,1)S(1)}) custom-call(s32[5]{0:T(128)S(1)} %stack.19.facts_ref, bf16[256,1024]{1,0:T(8,128)(2,1)S(1)} %copy-done.1, bf16[256,1024]{1,0:T(8,128)(2,1)S(1)} %copy-done.2, ...), custom_call_target="tpu_custom_call" | custom-call | tf_op jit(solution)/shard_map/pallas_call | solution.py:105
  62.6 2.3 %collective-permute-start.1 = (bf16[512,256]{1,0:T(8,128)(2,1)S(1)}, bf16[512,256]{1,0:T(8,128)(2,1)S(1)}, u32[]{:S(2)}, u32[]{:S(2)}) collective-permute-start(bf16[512,256]{1,0:T(8,128)(2,1)S(1)} %get-tuple-element.12), channel_id=1, source_target_pairs={{0,8},{8,0},{1,9},{9,1},{2,10},{10,2},{3,11},{11,3},{4,12},{12,4},... | collective-permute-start | bytes 786440 | tf_op jit(solution)/shard_map/ppermute | solution.py:207
  64.9 1.1 collective-permute-done.1.other_ref
  66.1 0.8 shard_map.88
  66.8 3.9 %all-to-all-start.2 = ((bf16[32,16,256]{2,1,0:T(8,128)(2,1)}), bf16[32,16,256]{2,1,0:T(8,128)(2,1)S(1)}, u32[]{:S(2)}, u32[]{:S(2)}) async-start(bf16[32,16,256]{2,1,0:T(8,128)(2,1)} %shard_map.88), calls=%async_computation.2 | async-start | bytes 524288 | tf_op jit(solution)/shard_map/all_to_all | solution.py:234
  70.7 8.0 %collective-permute-start.2 = (bf16[4,32,1280]{2,1,0:T(8,128)(2,1)S(1)}, bf16[4,32,1280]{2,1,0:T(8,128)(2,1)S(1)}, u32[]{:S(2)}, u32[]{:S(2)}) collective-permute-start(bf16[4,32,1280]{2,1,0:T(8,128)(2,1)S(1)} %get-tuple-element.14), channel_id=1, source_target_pairs={{0,1},{1,0},{2,3},{3,2},{4,5},{5,4},{6,7},{7,6},{8,9},{9,8},{10,11... | collective-permute-start | bytes 983048 | tf_op jit(solution)/shard_map/ppermute | solution.py:207
  78.7 14.5 %collective-permute-done.2.got_ref = bf16[4,32,1280]{2,1,0:T(8,128)(2,1)S(1)} collective-permute-done((bf16[4,32,1280]{2,1,0:T(8,128)(2,1)S(1)}, bf16[4,32,1280]{2,1,0:T(8,128)(2,1)S(1)}, u32[]{:S(2)}, u32[]{:S(2)}) %collective-permute-start.2) | collective-permute-done | bytes 327712 | tf_op jit(solution)/shard_map/ppermute | solution.py:207
  93.2 0.0 all-to-all-done.2.pieces_ref
  93.2 0.8 shard_map.89
  93.9 13.4 %all-to-all-start.3 = ((bf16[32,16,256]{2,1,0:T(8,128)(2,1)}), bf16[32,16,256]{2,1,0:T(8,128)(2,1)S(1)}, u32[]{:S(2)}, u32[]{:S(2)}) async-start(bf16[32,16,256]{2,1,0:T(8,128)(2,1)} %get-tuple-element.15), calls=%async_computation.3 | async-start | bytes 524288 | tf_op jit(solution)/shard_map/all_to_all | solution.py:201
  107.4 3.1 %collective-permute-start.3 = (bf16[2,32,1280]{2,1,0:T(8,128)(2,1)S(1)}, bf16[2,32,1280]{2,1,0:T(8,128)(2,1)S(1)}, u32[]{:S(2)}, u32[]{:S(2)}) collective-permute-start(bf16[2,32,1280]{2,1,0:T(8,128)(2,1)S(1)} %get-tuple-element.16), channel_id=1, source_target_pairs={{0,2},{1,3},{2,4},{3,5},{4,6},{5,7},{6,0},{7,1},{8,10},{9,11},{10,... | collective-permute-start | bytes 491528 | tf_op jit(solution)/shard_map/ppermute | solution.py:238
  110.5 4.4 %collective-permute-start.4 = (bf16[2,32,1280]{2,1,0:T(8,128)(2,1)S(1)}, bf16[2,32,1280]{2,1,0:T(8,128)(2,1)S(1)}, u32[]{:S(2)}, u32[]{:S(2)}) collective-permute-start(bf16[2,32,1280]{2,1,0:T(8,128)(2,1)S(1)} %get-tuple-element.17), channel_id=1, source_target_pairs={{0,4},{1,5},{2,6},{3,7},{4,0},{5,1},{6,2},{7,3},{8,12},{9,13},{10,... | collective-permute-start | bytes 491528 | tf_op jit(solution)/shard_map/ppermute | solution.py:238
  114.9 3.1 %collective-permute-start.5 = (bf16[2,32,1280]{2,1,0:T(8,128)(2,1)S(1)}, bf16[2,32,1280]{2,1,0:T(8,128)(2,1)S(1)}, u32[]{:S(2)}, u32[]{:S(2)}) collective-permute-start(bf16[2,32,1280]{2,1,0:T(8,128)(2,1)S(1)} %get-tuple-element.18), channel_id=1, source_target_pairs={{0,6},{1,7},{2,0},{3,1},{4,2},{5,3},{6,4},{7,5},{8,14},{9,15},{10,... | collective-permute-start | bytes 491528 | tf_op jit(solution)/shard_map/ppermute | solution.py:238
  117.9 0.0 all-to-all-done.3
  117.9 4.4 %all_gather.7.total_ref = bf16[1024,256]{1,0:T(8,128)(2,1)S(1)} all-gather(bf16[512,256]{1,0:T(8,128)(2,1)S(1)} %bitcast.12), channel_id=1, replica_groups=mesh['zl'=4,'y'=8,'core'=2,'kv'=8] {'core'}, dimensions={0}, use_global_device_ids=true | all-gather | bytes 786432 | tf_op jit(solution)/shard_map/all_gather | solution.py:202
  122.3 0.0 collective-permute-done.3.rest_0_
  122.3 0.0 collective-permute-done.4.rest_1_
  122.3 0.0 collective-permute-done.5.rest_2_
  122.3 1.7 %shard_map.90 = (bf16[32,8192]{1,0:T(8,128)(2,1)}, bf16[32,2048]{1,0:T(8,128)(2,1)}, bf16[1,1024,256]{2,1,0:T(8,128)(2,1)}) custom-call(s32[5]{0:T(128)S(1)} %stack.19.facts_ref, bf16[1024,256]{1,0:T(8,128)(2,1)S(1)} %all_gather.7.total_ref, bf16[4,32,1280]{2,1,0:T(8,128)(2,1)S(1)} %get-tuple-element.13.keep_ref, ...), custom_call_target="tpu_custom_call" | custom-call | tf_op jit(solution)/shard_map/pallas_call | solution.py:127
  (3 shorter events, 0.0 us)
Async XLA Ops:
  0.6 10.5 %collective-permute-start = (bf16[1024,256]{1,0:T(8,128)(2,1)}, bf16[1024,256]{1,0:T(8,128)(2,1)S(1)}, u32[]{:S(2)}, u32[]{:S(2)}) collective-permute-start(bf16[1024,256]{1,0:T(8,128)(2,1)} %bitcast.10), channel_id=1, source_target_pairs={{0,8},{8,0},{1,9},{9,1},{2,10},{10,2},{3,11},{11,3},{4,12},{12,4},... | collective-permute-start | bytes 1572872 | tf_op jit(solution)/shard_map/ppermute | solution.py:207
  11.2 1.0 copy-start
  30.6 21.7 %copy-start.2 = (bf16[256,1024]{1,0:T(8,128)(2,1)S(1)}, bf16[256,1024]{1,0:T(8,128)(2,1)}, u32[]{:S(2)}) copy-start(bf16[256,1024]{1,0:T(8,128)(2,1)} %grad_ref.1) | copy-start | bytes 1572868
  47.0 5.3 %copy-start.1 = (bf16[256,1024]{1,0:T(8,128)(2,1)S(1)}, bf16[256,1024]{1,0:T(8,128)(2,1)}, u32[]{:S(2)}) copy-start(bf16[256,1024]{1,0:T(8,128)(2,1)} %query_ref.1) | copy-start | bytes 1572868
  47.0 5.3 %copy-start.3 = (bf16[256,256]{1,0:T(8,128)(2,1)S(1)}, bf16[256,256]{1,0:T(8,128)(2,1)}, u32[]{:S(2)}) copy-start(bf16[256,256]{1,0:T(8,128)(2,1)} %cont_ref.1) | copy-start | bytes 393220
  62.6 3.4 %collective-permute-start.1 = (bf16[512,256]{1,0:T(8,128)(2,1)S(1)}, bf16[512,256]{1,0:T(8,128)(2,1)S(1)}, u32[]{:S(2)}, u32[]{:S(2)}) collective-permute-start(bf16[512,256]{1,0:T(8,128)(2,1)S(1)} %get-tuple-element.12), channel_id=1, source_target_pairs={{0,8},{8,0},{1,9},{9,1},{2,10},{10,2},{3,11},{11,3},{4,12},{12,4},... | collective-permute-start | bytes 786440 | tf_op jit(solution)/shard_map/ppermute | solution.py:207
  66.8 26.3 %all-to-all-start.2 = ((bf16[32,16,256]{2,1,0:T(8,128)(2,1)}), bf16[32,16,256]{2,1,0:T(8,128)(2,1)S(1)}, u32[]{:S(2)}, u32[]{:S(2)}) async-start(bf16[32,16,256]{2,1,0:T(8,128)(2,1)} %shard_map.88), calls=%async_computation.2 | async-start | bytes 524288 | tf_op jit(solution)/shard_map/all_to_all | solution.py:234
  70.7 22.4 %collective-permute-start.2 = (bf16[4,32,1280]{2,1,0:T(8,128)(2,1)S(1)}, bf16[4,32,1280]{2,1,0:T(8,128)(2,1)S(1)}, u32[]{:S(2)}, u32[]{:S(2)}) collective-permute-start(bf16[4,32,1280]{2,1,0:T(8,128)(2,1)S(1)} %get-tuple-element.14), channel_id=1, source_target_pairs={{0,1},{1,0},{2,3},{3,2},{4,5},{5,4},{6,7},{7,6},{8,9},{9,8},{10,11... | collective-permute-start | bytes 983048 | tf_op jit(solution)/shard_map/ppermute | solution.py:207
  93.9 24.0 %all-to-all-start.3 = ((bf16[32,16,256]{2,1,0:T(8,128)(2,1)}), bf16[32,16,256]{2,1,0:T(8,128)(2,1)S(1)}, u32[]{:S(2)}, u32[]{:S(2)}) async-start(bf16[32,16,256]{2,1,0:T(8,128)(2,1)} %get-tuple-element.15), calls=%async_computation.3 | async-start | bytes 524288 | tf_op jit(solution)/shard_map/all_to_all | solution.py:201
  107.4 14.9 %collective-permute-start.3 = (bf16[2,32,1280]{2,1,0:T(8,128)(2,1)S(1)}, bf16[2,32,1280]{2,1,0:T(8,128)(2,1)S(1)}, u32[]{:S(2)}, u32[]{:S(2)}) collective-permute-start(bf16[2,32,1280]{2,1,0:T(8,128)(2,1)S(1)} %get-tuple-element.16), channel_id=1, source_target_pairs={{0,2},{1,3},{2,4},{3,5},{4,6},{5,7},{6,0},{7,1},{8,10},{9,11},{10,... | collective-permute-start | bytes 491528 | tf_op jit(solution)/shard_map/ppermute | solution.py:238
  110.5 11.8 %collective-permute-start.4 = (bf16[2,32,1280]{2,1,0:T(8,128)(2,1)S(1)}, bf16[2,32,1280]{2,1,0:T(8,128)(2,1)S(1)}, u32[]{:S(2)}, u32[]{:S(2)}) collective-permute-start(bf16[2,32,1280]{2,1,0:T(8,128)(2,1)S(1)} %get-tuple-element.17), channel_id=1, source_target_pairs={{0,4},{1,5},{2,6},{3,7},{4,0},{5,1},{6,2},{7,3},{8,12},{9,13},{10,... | collective-permute-start | bytes 491528 | tf_op jit(solution)/shard_map/ppermute | solution.py:238
  114.9 7.5 %collective-permute-start.5 = (bf16[2,32,1280]{2,1,0:T(8,128)(2,1)S(1)}, bf16[2,32,1280]{2,1,0:T(8,128)(2,1)S(1)}, u32[]{:S(2)}, u32[]{:S(2)}) collective-permute-start(bf16[2,32,1280]{2,1,0:T(8,128)(2,1)S(1)} %get-tuple-element.18), channel_id=1, source_target_pairs={{0,6},{1,7},{2,0},{3,1},{4,2},{5,3},{6,4},{7,5},{8,14},{9,15},{10,... | collective-permute-start | bytes 491528 | tf_op jit(solution)/shard_map/ppermute | solution.py:238

commit v4 on v3

--- a/solution.py
+++ b/solution.py
@@ -26,14 +26,14 @@
 
 
 def attention_kernel(
-    facts_ref, query_ref, grad_ref, prompt_ref, cont_ref, own_ref, other_ref, keep_ref,
-    give_ref, key_ref, value_ref, turned_ref, dk_ref, dv_ref
+    facts_ref, query_ref, grad_ref, prompt_ref, cont_ref, own_ref, other_ref, *rest
 ):
     tokens, width = query_ref.shape
     prompt_len = prompt_ref.shape[0]
     hd = cont_ref.shape[1] // 2
     heads = width // hd
-    ring, share, _ = keep_ref.shape
+    *token_refs, key_ref, value_ref, turned_ref, dk_ref, dv_ref, block_ref = rest
+    ring, _, share, _ = block_ref.shape
     around, side = facts_ref[KV] // 2, facts_ref[KV] % 2
     scale = 1.0 / math.sqrt(hd)
     key_ref[:prompt_len] = prompt_ref[:, :hd]
@@ -46,28 +46,31 @@
         jnp.int32, (tokens, tokens), 1
     )
 
-    def hand_out(grads, columns):
-        blocks = grads.reshape(ring, 2, share, hd)
-        same = jnp.full((share, hd), side, jnp.int32) == 0
-        for x in range(ring):
-            distance = (x - around + ring) % ring
-            low, high = blocks[x, 0], blocks[x, 1]
-            keep_ref[distance, :, columns] = jnp.where(same, low, high)
-            give_ref[distance, :, columns] = jnp.where(same, high, low)
+    def inputs(head):
+        cols = slice(head * hd, (head + 1) * hd)
+        return query_ref[:, cols], jnp.where(live, grad_ref[:, cols], jnp.zeros((), jnp.bfloat16))
 
     def products(head):
-        cols = slice(head * hd, (head + 1) * hd)
-        q = query_ref[:, cols]
-        g = jnp.where(live, grad_ref[:, cols], jnp.zeros((), jnp.bfloat16))
+        q, g = inputs(head)
         s = dot(key_ref[...], q, NT)
         s = jnp.concatenate([s[:prompt_len], jnp.where(causal, s[prompt_len:], -1e30)], 0)
         return q, g, s, dot(value_ref[...], g, NT)
 
-    ahead = products(0)
-    for head in range(heads):
-        q, g, s, d = ahead
-        if head + 1 < heads:
-            ahead = products(head + 1)
+    def add_up(head, dk, dv):
+        if head == 0:
+            dk_ref[...] = dk
+            dv_ref[...] = dv
+        else:
+            dk_ref[...] += dk
+            dv_ref[...] += dv
+
+    def store_query(head, dq):
+        block_ref[..., head * hd : (head + 1) * hd] = dq.astype(jnp.bfloat16).reshape(
+            ring, 2, share, hd
+        )
+
+    def shifted(head):
+        q, g, s, d = products(head)
         top = jnp.max(s, axis=0, keepdims=True) * (scale * LOG2E)
         e = jnp.exp2(s * (scale * LOG2E) - top)
         inv = 1.0 / jnp.sum(e, axis=0, keepdims=True)
@@ -75,25 +78,44 @@
         probs = e * inv
         w = probs.astype(jnp.bfloat16)
         ds = (probs * (d - delta) * scale).astype(jnp.bfloat16)
-        dk = dot(ds, q)
-        dv = dot(w, g)
-        if head == 0:
-            dk_ref[...] = dk
-            dv_ref[...] = dv
-        else:
-            dk_ref[...] += dk
-            dv_ref[...] += dv
-        dq = dot(turned_ref[...], ds).T.astype(jnp.bfloat16)
-        hand_out(dq, slice(head * hd, (head + 1) * hd))
+        add_up(head, dot(ds, q), dot(w, g))
+        store_query(head, dot(turned_ref[...], ds).T)
+
+    least, most = None, None
+    ahead = products(0)
+    for head in range(heads):
+        q, g, s, d = ahead
+        if head + 1 < heads:
+            ahead = products(head + 1)
+        e = jnp.exp2(s * (scale * LOG2E))
+        total = jnp.sum(e, axis=0, keepdims=True)
+        inv = 1.0 / total
+        delta = jnp.sum(e * d, axis=0, keepdims=True) * inv
+        probs = e * inv
+        w = probs.astype(jnp.bfloat16)
+        ds = (probs * (d - delta) * scale).astype(jnp.bfloat16)
+        add_up(head, dot(ds, q), dot(w, g))
+        store_query(head, dot(turned_ref[...], ds).T)
+        least = total if head == 0 else jnp.minimum(least, total)
+        most = total if head == 0 else jnp.maximum(most, total)
+    safe = (jnp.min(least) > 2.0**-60) & (jnp.max(most) < 2.0**60)
+
+    @pl.when(jnp.logical_not(safe))
+    def _():
+        for head in range(heads):
+            shifted(head)
+
     half = prompt_len // 2
     mine = pl.ds(pl.multiple_of(facts_ref[CORE] * half, half), half)
     theirs = pl.ds(pl.multiple_of((1 - facts_ref[CORE]) * half, half), half)
     for ref, first in ((dk_ref, 0), (dv_ref, hd)):
         own_ref[:, first : first + hd] = ref[mine]
         other_ref[:, first : first + hd] = ref[theirs].astype(jnp.bfloat16)
-        hand_out(
-            ref[prompt_len:].astype(jnp.bfloat16), slice(width + first, width + first + hd)
-        )
+        grads = ref[prompt_len:].astype(jnp.bfloat16)
+        block_ref[..., width + first : width + first + hd] = grads.reshape(ring, 2, share, hd)
+    for distance, token_ref in enumerate(token_refs):
+        for slot in range(2):
+            token_ref[slot] = block_ref[(around + distance) % ring, (side + slot) % 2]
 
 
 def attention_grads(query, grad, prompt, cont, facts, ring):
@@ -101,23 +123,24 @@
     prompt_len, both = prompt.shape
     hd = both // 2
     keys = prompt_len + tokens
-    blocks = like((ring, tokens // ring // 2, width + both))
+    share = tokens // ring // 2
+    blocks = like((2, share, width + both))
     return pl.pallas_call(
         attention_kernel,
         out_shape=(
             like((prompt_len // 2, both), jnp.float32),
             like((prompt_len // 2, both)),
-            blocks,
-            blocks,
+            *[blocks] * ring,
         ),
         in_specs=[SMEM] + [VMEM] * 4,
-        out_specs=[VMEM] * 4,
+        out_specs=[VMEM] * (2 + ring),
         scratch_shapes=[
             pltpu.VMEM((keys, hd), jnp.bfloat16),
             pltpu.VMEM((keys, hd), jnp.bfloat16),
             pltpu.VMEM((hd, keys), jnp.bfloat16),
             pltpu.VMEM((keys, hd), jnp.float32),
             pltpu.VMEM((keys, hd), jnp.float32),
+            pltpu.VMEM((ring, 2, share, width + both), jnp.bfloat16),
         ],
         compiler_params=pltpu.CompilerParams(vmem_limit_bytes=48 * 2**20),
     )(facts, query, grad, prompt, cont)
@@ -161,28 +184,27 @@
     pieces_ref[...] = half.astype(jnp.bfloat16).reshape(pieces_ref.shape)
 
 
-def sum_pieces(pieces_ref, keep_ref, got_ref, copies_ref, *sends):
-    for distance, send in enumerate(sends):
-        send[0] = keep_ref[distance + 1]
-        send[1] = got_ref[distance + 1]
+def sum_pieces(pieces_ref, *rest):
+    came, (copies_ref, give_ref) = rest[:-2], rest[-2:]
+    for distance, block in enumerate(came):
+        give_ref[distance] = block[1]
     piece = jnp.sum(pieces_ref[...].astype(jnp.float32), axis=0).astype(jnp.bfloat16)
     for peer in range(copies_ref.shape[0]):
         copies_ref[peer] = piece
 
 
-def finish(facts_ref, total_ref, keep_ref, got_ref, *rest):
+def finish(facts_ref, total_ref, got_ref, *rest):
     came, (query_ref, cont_ref, prompt_ref) = rest[:-3], rest[-3:]
-    ring, _, width = keep_ref.shape
+    ring, _, width = got_ref.shape
     cont = cont_ref.shape[1] // (2 * ring)
     size = width - cont
     around, side = facts_ref[KV] // 2, facts_ref[KV] % 2
     for distance in range(ring):
-        for slot in range(2):
-            if distance:
-                block = came[distance - 1].at[slot]
-            else:
-                block = (keep_ref, got_ref)[slot].at[0]
-            head = (around - distance + ring) % ring * 2 + (side if slot == 0 else 1 - side)
+        source = (around - distance + ring) % ring * 2
+        for block, head in (
+            (came[distance].at[0], source + side),
+            (got_ref.at[distance], source + 1 - side),
+        ):
             for ref, first, count in ((query_ref, 0, size), (cont_ref, size, cont)):
                 columns = pl.ds(pl.multiple_of(head * count, count), count)
                 ref[:, columns] = block[:, first : first + count]
@@ -227,17 +249,17 @@
     copies = local_call(pick_piece, pieces, facts, found, places=[SMEM, VMEM])
     shared = collect(copies)
 
-    own, other, keep, give = attention_grads(query, out_grad, shared, cont_kv, facts, ring)
-    other = swap(other, "core")
+    own, other, *blocks = attention_grads(query, out_grad, shared, cont_kv, facts, ring)
+    came = [blocks[0]] + [
+        lax.ppermute(block, "kv", [(i, (i + 2 * n) % heads) for i in range(heads)])
+        for n, block in enumerate(blocks)
+        if n
+    ]
+    parts = local_call(add_halves, pieces, own, swap(other, "core"))
+    parts = lax.all_to_all(parts, CHIPS, 0, 0, tiled=True)
+    give = like((ring, *blocks[0].shape[1:]))
+    copies, give = local_call(sum_pieces, (pieces, give), parts, *came)
     got = swap(give, "kv")
-    parts = local_call(add_halves, pieces, own, other)
-    parts = lax.all_to_all(parts, CHIPS, 0, 0, tiled=True)
-    send = like((2, *keep.shape[1:]))
-    copies, *sends = local_call(sum_pieces, (pieces, *[send] * (ring - 1)), parts, keep, got)
-    came = [
-        lax.ppermute(block, "kv", [(i, (i + 2 * (n + 1)) % heads) for i in range(heads)])
-        for n, block in enumerate(sends)
-    ]
     total = collect(copies)
     outs = (
         like((tokens // heads, heads * width)),
@@ -245,7 +267,7 @@
         like((1, rows, both)),
     )
     return local_call(
-        finish, outs, facts, total, keep, got, *came, places=[SMEM] + [VMEM] * (ring + 2)
+        finish, outs, facts, total, got, *came, places=[SMEM] + [VMEM] * (ring + 2)
     )
 
 

time: 125 us -> 133 us (1.064)
  the two profiles are of different devices: /device:TPU:1 before, /device:TPU:194 now
where the time goes in v4:
time: 133 us; the launch traced here: 132 us
  blocking collectives  42 us (32%)
  starting transfers between devices  39 us (29%)
  Pallas kernels  24.1 us (18%)
  waiting for transfers between devices  23.8 us (18%)
  between operations  2.05 us (2%)
    all_to_all x1, blocking collectives, body(): found = lax.all_to_all(half.reshape(pieces.shape), CHIPS, 0, 0, tiled=True)  21.1 us
    pallas_call x1, Pallas kernels, attention_grads(): pl.pallas_call(attention_kernel, out_shape=(like((prompt_len // 2, both),...  19.8 us
    ppermute x3, waiting for transfers between devices, swap(): return lax.ppermute(block, axis, pairs)  16.5 us
    all_to_all x1, blocking collectives, collect(): half = lax.all_to_all(copies, CHIPS, 0, 0, tiled=True)  16.4 us
    ppermute x3, starting transfers between devices, swap(): return lax.ppermute(block, axis, pairs)  12.2 us
    ppermute x3, starting transfers between devices, body(): lax.ppermute(block, 'kv', [(i, (i + 2 * n) % heads) for i in range(heads)])  10.5 us
    all_to_all x1, starting transfers between devices, collect(): half = lax.all_to_all(copies, CHIPS, 0, 0, tiled=True)  10.1 us
    all_to_all x1, starting transfers between devices, body(): parts = lax.all_to_all(parts, CHIPS, 0, 0, tiled=True)  6.2 us
  transfers between devices with their start and end apart: 8, of which 6 were waited for; matrix products, arithmetic and copies ran while one was open for 0% of the time, Pallas kernels for 0%

profile of v4, /device:TPU:194, one launch (start us, length us, event | category | flops | bytes accessed | tf_op | source)
XLA Modules:
  0.0 132.0 jit_solution(3904155971830351974)
XLA Ops:
  0.6 1.9 %collective-permute-start = (bf16[1024,256]{1,0:T(8,128)(2,1)}, bf16[1024,256]{1,0:T(8,128)(2,1)S(1)}, u32[]{:S(2)}, u32[]{:S(2)}) collective-permute-start(bf16[1024,256]{1,0:T(8,128)(2,1)} %bitcast.10), channel_id=1, source_target_pairs={{0,8},{8,0},{1,9},{9,1},{2,10},{10,2},{3,11},{11,3},{4,12},{12,4},... | collective-permute-start | bytes 1572872 | tf_op jit(solution)/shard_map/ppermute | solution.py:229
  3.9 0.1 stack.19.facts_ref
  3.9 0.7 collective-permute-done.other_ref
  4.6 1.0 copy-done
  5.7 0.6 shard_map.85
  6.3 21.1 %all_to_all.20.pieces_ref = bf16[32,16,256]{2,1,0:T(8,128)(2,1)S(1)} all-to-all(bf16[32,16,256]{2,1,0:T(8,128)(2,1)S(1)} %bitcast.9), channel_id=1, replica_groups=mesh['zl'=4,'y'=8,'core'=2,'kv'=8] {'zl','y'}, dimensions={0} | all-to-all | bytes 524288 | tf_op jit(solution)/shard_map/all_to_all | solution.py:248
  27.4 0.6 shard_map.86
  27.9 0.0 copy-start.2
  27.9 16.4 %all_to_all.21 = bf16[32,16,256]{2,1,0:T(8,128)(2,1)S(1)} all-to-all(bf16[32,16,256]{2,1,0:T(8,128)(2,1)S(1)} %shard_map.86), channel_id=1, replica_groups=mesh['zl'=4,'y'=8,'core'=2,'kv'=8] {'zl','y'}, dimensions={0} | all-to-all | bytes 524288 | tf_op jit(solution)/shard_map/all_to_all | solution.py:223
  44.4 2.3 %all_gather.6.prompt_ref = bf16[1024,256]{1,0:T(8,128)(2,1)S(1)} all-gather(bf16[512,256]{1,0:T(8,128)(2,1)S(1)} %bitcast.13), channel_id=1, replica_groups=mesh['zl'=4,'y'=8,'core'=2,'kv'=8] {'core'}, dimensions={0}, use_global_device_ids=true | all-gather | bytes 786432 | tf_op jit(solution)/shard_map/all_gather | solution.py:224
  46.7 0.0 copy-done.2
  46.7 0.0 copy-done.1
  46.7 0.0 copy-done.3
  46.7 19.8 %shard_map.87 = (f32[512,256]{1,0:T(8,128)S(1)}, bf16[512,256]{1,0:T(8,128)(2,1)S(1)}, bf16[2,32,1280]{2,1,0:T(8,128)(2,1)S(1)}, bf16[2,32,1280]{2,1,0:T(8,128)(...) custom-call(s32[5]{0:T(128)S(1)} %stack.19.facts_ref, bf16[256,1024]{1,0:T(8,128)(2,1)S(1)} %copy-done.1, ...), custom_call_target="tpu_custom_call" | custom-call | tf_op jit(solution)/shard_map/pallas_call | solution.py:128
  66.5 2.0 %collective-permute-start.1 = (bf16[512,256]{1,0:T(8,128)(2,1)S(1)}, bf16[512,256]{1,0:T(8,128)(2,1)S(1)}, u32[]{:S(2)}, u32[]{:S(2)}) collective-permute-start(bf16[512,256]{1,0:T(8,128)(2,1)S(1)} %get-tuple-element.12), channel_id=1, source_target_pairs={{0,8},{8,0},{1,9},{9,1},{2,10},{10,2},{3,11},{11,3},{4,12},{12,4},... | collective-permute-start | bytes 786440 | tf_op jit(solution)/shard_map/ppermute | solution.py:229
  68.5 1.4 %collective-permute-done.1.other_ref = bf16[512,256]{1,0:T(8,128)(2,1)S(1)} collective-permute-done((bf16[512,256]{1,0:T(8,128)(2,1)S(1)}, bf16[512,256]{1,0:T(8,128)(2,1)S(1)}, u32[]{:S(2)}, u32[]{:S(2)}) %collective-permute-start.1) | collective-permute-done | bytes 262176 | tf_op jit(solution)/shard_map/ppermute | solution.py:229
  69.9 0.8 shard_map.88
  70.7 6.2 %all-to-all-start.2 = ((bf16[32,16,256]{2,1,0:T(8,128)(2,1)}), bf16[32,16,256]{2,1,0:T(8,128)(2,1)S(1)}, u32[]{:S(2)}, u32[]{:S(2)}) async-start(bf16[32,16,256]{2,1,0:T(8,128)(2,1)} %shard_map.88), calls=%async_computation.2 | async-start | bytes 524288 | tf_op jit(solution)/shard_map/all_to_all | solution.py:259
  76.9 3.4 %collective-permute-start.2 = (bf16[2,32,1280]{2,1,0:T(8,128)(2,1)S(1)}, bf16[2,32,1280]{2,1,0:T(8,128)(2,1)S(1)}, u32[]{:S(2)}, u32[]{:S(2)}) collective-permute-start(bf16[2,32,1280]{2,1,0:T(8,128)(2,1)S(1)} %get-tuple-element.14), channel_id=1, source_target_pairs={{0,2},{1,3},{2,4},{3,5},{4,6},{5,7},{6,0},{7,1},{8,10},{9,11},{10,... | collective-permute-start | bytes 491528 | tf_op jit(solution)/shard_map/ppermute | solution.py:254
  80.3 3.0 %collective-permute-start.3 = (bf16[2,32,1280]{2,1,0:T(8,128)(2,1)S(1)}, bf16[2,32,1280]{2,1,0:T(8,128)(2,1)S(1)}, u32[]{:S(2)}, u32[]{:S(2)}) collective-permute-start(bf16[2,32,1280]{2,1,0:T(8,128)(2,1)S(1)} %get-tuple-element.15), channel_id=1, source_target_pairs={{0,4},{1,5},{2,6},{3,7},{4,0},{5,1},{6,2},{7,3},{8,12},{9,13},{10,... | collective-permute-start | bytes 491528 | tf_op jit(solution)/shard_map/ppermute | solution.py:254
  83.3 4.1 %collective-permute-start.4 = (bf16[2,32,1280]{2,1,0:T(8,128)(2,1)S(1)}, bf16[2,32,1280]{2,1,0:T(8,128)(2,1)S(1)}, u32[]{:S(2)}, u32[]{:S(2)}) collective-permute-start(bf16[2,32,1280]{2,1,0:T(8,128)(2,1)S(1)} %get-tuple-element.16), channel_id=1, source_target_pairs={{0,6},{1,7},{2,0},{3,1},{4,2},{5,3},{6,4},{7,5},{8,14},{9,15},{10,... | collective-permute-start | bytes 491528 | tf_op jit(solution)/shard_map/ppermute | solution.py:254
  87.4 0.0 collective-permute-done.2.rest_1_
  87.4 3.4 %collective-permute-done.3.rest_2_ = bf16[2,32,1280]{2,1,0:T(8,128)(2,1)S(1)} collective-permute-done((bf16[2,32,1280]{2,1,0:T(8,128)(2,1)S(1)}, bf16[2,32,1280]{2,1,0:T(8,128)(2,1)S(1)}, u32[]{:S(2)}, u32[]{:S(2)}) %collective-permute-start.3) | collective-permute-done | bytes 163872 | tf_op jit(solution)/shard_map/ppermute | solution.py:254
  90.8 1.9 %collective-permute-done.4.rest_3_ = bf16[2,32,1280]{2,1,0:T(8,128)(2,1)S(1)} collective-permute-done((bf16[2,32,1280]{2,1,0:T(8,128)(2,1)S(1)}, bf16[2,32,1280]{2,1,0:T(8,128)(2,1)S(1)}, u32[]{:S(2)}, u32[]{:S(2)}) %collective-permute-start.4) | collective-permute-done | bytes 163872 | tf_op jit(solution)/shard_map/ppermute | solution.py:254
  92.7 0.0 all-to-all-done.2.pieces_ref
  92.7 0.8 shard_map.89
  93.5 10.1 %all-to-all-start.3 = ((bf16[32,16,256]{2,1,0:T(8,128)(2,1)}), bf16[32,16,256]{2,1,0:T(8,128)(2,1)S(1)}, u32[]{:S(2)}, u32[]{:S(2)}) async-start(bf16[32,16,256]{2,1,0:T(8,128)(2,1)} %get-tuple-element.17), calls=%async_computation.3 | async-start | bytes 524288 | tf_op jit(solution)/shard_map/all_to_all | solution.py:223
  103.6 8.2 %collective-permute-start.5 = (bf16[4,32,1280]{2,1,0:T(8,128)(2,1)S(1)}, bf16[4,32,1280]{2,1,0:T(8,128)(2,1)S(1)}, u32[]{:S(2)}, u32[]{:S(2)}) collective-permute-start(bf16[4,32,1280]{2,1,0:T(8,128)(2,1)S(1)} %get-tuple-element.18), channel_id=1, source_target_pairs={{0,1},{1,0},{2,3},{3,2},{4,5},{5,4},{6,7},{7,6},{8,9},{9,8},{10,11... | collective-permute-start | bytes 983048 | tf_op jit(solution)/shard_map/ppermute | solution.py:229
  111.9 1.9 %all-to-all-done.3 = bf16[32,16,256]{2,1,0:T(8,128)(2,1)S(1)} async-done(((bf16[32,16,256]{2,1,0:T(8,128)(2,1)}), bf16[32,16,256]{2,1,0:T(8,128)(2,1)S(1)}, u32[]{:S(2)}, u32[]{:S(2)}) %all-to-all-start.3) | async-done | bytes 262176 | tf_op jit(solution)/shard_map/all_to_all | solution.py:223
  113.8 2.2 %all_gather.7.total_ref = bf16[1024,256]{1,0:T(8,128)(2,1)S(1)} all-gather(bf16[512,256]{1,0:T(8,128)(2,1)S(1)} %bitcast.12), channel_id=1, replica_groups=mesh['zl'=4,'y'=8,'core'=2,'kv'=8] {'core'}, dimensions={0}, use_global_device_ids=true | all-gather | bytes 786432 | tf_op jit(solution)/shard_map/all_gather | solution.py:224
  116.0 14.4 %collective-permute-done.5.got_ref = bf16[4,32,1280]{2,1,0:T(8,128)(2,1)S(1)} collective-permute-done((bf16[4,32,1280]{2,1,0:T(8,128)(2,1)S(1)}, bf16[4,32,1280]{2,1,0:T(8,128)(2,1)S(1)}, u32[]{:S(2)}, u32[]{:S(2)}) %collective-permute-start.5) | collective-permute-done | bytes 327712 | tf_op jit(solution)/shard_map/ppermute | solution.py:229
  130.4 1.6 %shard_map.90 = (bf16[32,8192]{1,0:T(8,128)(2,1)}, bf16[32,2048]{1,0:T(8,128)(2,1)}, bf16[1,1024,256]{2,1,0:T(8,128)(2,1)}) custom-call(s32[5]{0:T(128)S(1)} %stack.19.facts_ref, bf16[1024,256]{1,0:T(8,128)(2,1)S(1)} %all_gather.7.total_ref, bf16[4,32,1280]{2,1,0:T(8,128)(2,1)S(1)} %collective-permute-done.5.got_ref, ...), custom_call_target="tpu_custom_call" | custom-call | tf_op jit(solution)/shard_map/pallas_call | solution.py:150
  (3 shorter events, 0.0 us)
Async XLA Ops:
  0.6 4.0 %collective-permute-start = (bf16[1024,256]{1,0:T(8,128)(2,1)}, bf16[1024,256]{1,0:T(8,128)(2,1)S(1)}, u32[]{:S(2)}, u32[]{:S(2)}) collective-permute-start(bf16[1024,256]{1,0:T(8,128)(2,1)} %bitcast.10), channel_id=1, source_target_pairs={{0,8},{8,0},{1,9},{9,1},{2,10},{10,2},{3,11},{11,3},{4,12},{12,4},... | collective-permute-start | bytes 1572872 | tf_op jit(solution)/shard_map/ppermute | solution.py:229
  4.6 1.0 copy-start
  27.9 18.7 %copy-start.2 = (bf16[256,1024]{1,0:T(8,128)(2,1)S(1)}, bf16[256,1024]{1,0:T(8,128)(2,1)}, u32[]{:S(2)}) copy-start(bf16[256,1024]{1,0:T(8,128)(2,1)} %grad_ref.1) | copy-start | bytes 1572868
  44.4 2.3 %copy-start.1 = (bf16[256,1024]{1,0:T(8,128)(2,1)S(1)}, bf16[256,1024]{1,0:T(8,128)(2,1)}, u32[]{:S(2)}) copy-start(bf16[256,1024]{1,0:T(8,128)(2,1)} %query_ref.1) | copy-start | bytes 1572868
  44.4 2.3 %copy-start.3 = (bf16[256,256]{1,0:T(8,128)(2,1)S(1)}, bf16[256,256]{1,0:T(8,128)(2,1)}, u32[]{:S(2)}) copy-start(bf16[256,256]{1,0:T(8,128)(2,1)} %cont_ref.1) | copy-start | bytes 393220
  66.5 3.4 %collective-permute-start.1 = (bf16[512,256]{1,0:T(8,128)(2,1)S(1)}, bf16[512,256]{1,0:T(8,128)(2,1)S(1)}, u32[]{:S(2)}, u32[]{:S(2)}) collective-permute-start(bf16[512,256]{1,0:T(8,128)(2,1)S(1)} %get-tuple-element.12), channel_id=1, source_target_pairs={{0,8},{8,0},{1,9},{9,1},{2,10},{10,2},{3,11},{11,3},{4,12},{12,4},... | collective-permute-start | bytes 786440 | tf_op jit(solution)/shard_map/ppermute | solution.py:229
  70.7 22.0 %all-to-all-start.2 = ((bf16[32,16,256]{2,1,0:T(8,128)(2,1)}), bf16[32,16,256]{2,1,0:T(8,128)(2,1)S(1)}, u32[]{:S(2)}, u32[]{:S(2)}) async-start(bf16[32,16,256]{2,1,0:T(8,128)(2,1)} %shard_map.88), calls=%async_computation.2 | async-start | bytes 524288 | tf_op jit(solution)/shard_map/all_to_all | solution.py:259
  76.9 10.5 %collective-permute-start.2 = (bf16[2,32,1280]{2,1,0:T(8,128)(2,1)S(1)}, bf16[2,32,1280]{2,1,0:T(8,128)(2,1)S(1)}, u32[]{:S(2)}, u32[]{:S(2)}) collective-permute-start(bf16[2,32,1280]{2,1,0:T(8,128)(2,1)S(1)} %get-tuple-element.14), channel_id=1, source_target_pairs={{0,2},{1,3},{2,4},{3,5},{4,6},{5,7},{6,0},{7,1},{8,10},{9,11},{10,... | collective-permute-start | bytes 491528 | tf_op jit(solution)/shard_map/ppermute | solution.py:254
  80.3 10.5 %collective-permute-start.3 = (bf16[2,32,1280]{2,1,0:T(8,128)(2,1)S(1)}, bf16[2,32,1280]{2,1,0:T(8,128)(2,1)S(1)}, u32[]{:S(2)}, u32[]{:S(2)}) collective-permute-start(bf16[2,32,1280]{2,1,0:T(8,128)(2,1)S(1)} %get-tuple-element.15), channel_id=1, source_target_pairs={{0,4},{1,5},{2,6},{3,7},{4,0},{5,1},{6,2},{7,3},{8,12},{9,13},{10,... | collective-permute-start | bytes 491528 | tf_op jit(solution)/shard_map/ppermute | solution.py:254
  83.3 9.4 %collective-permute-start.4 = (bf16[2,32,1280]{2,1,0:T(8,128)(2,1)S(1)}, bf16[2,32,1280]{2,1,0:T(8,128)(2,1)S(1)}, u32[]{:S(2)}, u32[]{:S(2)}) collective-permute-start(bf16[2,32,1280]{2,1,0:T(8,128)(2,1)S(1)} %get-tuple-element.16), channel_id=1, source_target_pairs={{0,6},{1,7},{2,0},{3,1},{4,2},{5,3},{6,4},{7,5},{8,14},{9,15},{10,... | collective-permute-start | bytes 491528 | tf_op jit(solution)/shard_map/ppermute | solution.py:254
  93.5 20.3 %all-to-all-start.3 = ((bf16[32,16,256]{2,1,0:T(8,128)(2,1)}), bf16[32,16,256]{2,1,0:T(8,128)(2,1)S(1)}, u32[]{:S(2)}, u32[]{:S(2)}) async-start(bf16[32,16,256]{2,1,0:T(8,128)(2,1)} %get-tuple-element.17), calls=%async_computation.3 | async-start | bytes 524288 | tf_op jit(solution)/shard_map/all_to_all | solution.py:223
  103.6 26.8 %collective-permute-start.5 = (bf16[4,32,1280]{2,1,0:T(8,128)(2,1)S(1)}, bf16[4,32,1280]{2,1,0:T(8,128)(2,1)S(1)}, u32[]{:S(2)}, u32[]{:S(2)}) collective-permute-start(bf16[4,32,1280]{2,1,0:T(8,128)(2,1)S(1)} %get-tuple-element.18), channel_id=1, source_target_pairs={{0,1},{1,0},{2,3},{3,2},{4,5},{5,4},{6,7},{7,6},{8,9},{9,8},{10,11... | collective-permute-start | bytes 983048 | tf_op jit(solution)/shard_map/ppermute | solution.py:229

commit v5 on v4

--- a/solution.py
+++ b/solution.py
@@ -113,9 +113,9 @@
         other_ref[:, first : first + hd] = ref[theirs].astype(jnp.bfloat16)
         grads = ref[prompt_len:].astype(jnp.bfloat16)
         block_ref[..., width + first : width + first + hd] = grads.reshape(ring, 2, share, hd)
-    for distance, token_ref in enumerate(token_refs):
-        for slot in range(2):
-            token_ref[slot] = block_ref[(around + distance) % ring, (side + slot) % 2]
+    for slot, token_ref in enumerate(token_refs):
+        for distance in range(ring):
+            token_ref[distance] = block_ref[(around + distance) % ring, (side + slot) % 2]
 
 
 def attention_grads(query, grad, prompt, cont, facts, ring):
@@ -124,16 +124,17 @@
     hd = both // 2
     keys = prompt_len + tokens
     share = tokens // ring // 2
-    blocks = like((2, share, width + both))
+    blocks = like((ring, share, width + both))
     return pl.pallas_call(
         attention_kernel,
         out_shape=(
             like((prompt_len // 2, both), jnp.float32),
             like((prompt_len // 2, both)),
-            *[blocks] * ring,
+            blocks,
+            blocks,
         ),
         in_specs=[SMEM] + [VMEM] * 4,
-        out_specs=[VMEM] * (2 + ring),
+        out_specs=[VMEM] * 4,
         scratch_shapes=[
             pltpu.VMEM((keys, hd), jnp.bfloat16),
             pltpu.VMEM((keys, hd), jnp.bfloat16),
@@ -184,27 +185,28 @@
     pieces_ref[...] = half.astype(jnp.bfloat16).reshape(pieces_ref.shape)
 
 
-def sum_pieces(pieces_ref, *rest):
-    came, (copies_ref, give_ref) = rest[:-2], rest[-2:]
-    for distance, block in enumerate(came):
-        give_ref[distance] = block[1]
+def sum_pieces(pieces_ref, keep_ref, got_ref, copies_ref, *sends):
+    for distance, send in enumerate(sends):
+        send[0] = keep_ref[distance + 1]
+        send[1] = got_ref[distance + 1]
     piece = jnp.sum(pieces_ref[...].astype(jnp.float32), axis=0).astype(jnp.bfloat16)
     for peer in range(copies_ref.shape[0]):
         copies_ref[peer] = piece
 
 
-def finish(facts_ref, total_ref, got_ref, *rest):
+def finish(facts_ref, total_ref, keep_ref, got_ref, *rest):
     came, (query_ref, cont_ref, prompt_ref) = rest[:-3], rest[-3:]
-    ring, _, width = got_ref.shape
+    ring, _, width = keep_ref.shape
     cont = cont_ref.shape[1] // (2 * ring)
     size = width - cont
     around, side = facts_ref[KV] // 2, facts_ref[KV] % 2
     for distance in range(ring):
-        source = (around - distance + ring) % ring * 2
-        for block, head in (
-            (came[distance].at[0], source + side),
-            (got_ref.at[distance], source + 1 - side),
-        ):
+        for slot in range(2):
+            if distance:
+                block = came[distance - 1].at[slot]
+            else:
+                block = (keep_ref, got_ref)[slot].at[0]
+            head = (around - distance + ring) % ring * 2 + (side if slot == 0 else 1 - side)
             for ref, first, count in ((query_ref, 0, size), (cont_ref, size, cont)):
                 columns = pl.ds(pl.multiple_of(head * count, count), count)
                 ref[:, columns] = block[:, first : first + count]
@@ -249,17 +251,21 @@
     copies = local_call(pick_piece, pieces, facts, found, places=[SMEM, VMEM])
     shared = collect(copies)
 
-    own, other, *blocks = attention_grads(query, out_grad, shared, cont_kv, facts, ring)
-    came = [blocks[0]] + [
-        lax.ppermute(block, "kv", [(i, (i + 2 * n) % heads) for i in range(heads)])
-        for n, block in enumerate(blocks)
-        if n
+    own, other, keep, give = attention_grads(query, out_grad, shared, cont_kv, facts, ring)
+    got = swap(give, "kv")
+    parts = local_call(add_halves, pieces, own, swap(other, "core"))
+    parts = lax.fori_loop(
+        0,
+        jnp.minimum(lengths[0], 1),
+        lambda _, block: lax.all_to_all(block, CHIPS, 0, 0, tiled=True),
+        parts,
+    )
+    send = like((2, *keep.shape[1:]))
+    copies, *sends = local_call(sum_pieces, (pieces, *[send] * (ring - 1)), parts, keep, got)
+    came = [
+        lax.ppermute(block, "kv", [(i, (i + 2 * (n + 1)) % heads) for i in range(heads)])
+        for n, block in enumerate(sends)
     ]
-    parts = local_call(add_halves, pieces, own, swap(other, "core"))
-    parts = lax.all_to_all(parts, CHIPS, 0, 0, tiled=True)
-    give = like((ring, *blocks[0].shape[1:]))
-    copies, give = local_call(sum_pieces, (pieces, give), parts, *came)
-    got = swap(give, "kv")
     total = collect(copies)
     outs = (
         like((tokens // heads, heads * width)),
@@ -267,7 +273,7 @@
         like((1, rows, both)),
     )
     return local_call(
-        finish, outs, facts, total, got, *came, places=[SMEM] + [VMEM] * (ring + 2)
+        finish, outs, facts, total, keep, got, *came, places=[SMEM] + [VMEM] * (ring + 2)
     )
 
 

time: 133 us -> 125 us (0.940)
  the two profiles are of different devices: /device:TPU:194 before, /device:TPU:1 now
where the time goes in v5:
time: 125 us
  blocking collectives  43.6 us (35%)
  starting transfers between devices  39.2 us (31%)
  Pallas kernels  25.1 us (20%)
  waiting for transfers between devices  13 us (10%)
  between operations  2.05 us (2%)
  local copies, waits for them, and re-layouts  1.84 us (1%)
    pallas_call x1, Pallas kernels, attention_grads(): pl.pallas_call(attention_kernel, out_shape=(like((prompt_len // 2, both),...  19.8 us
    ppermute x3, starting transfers between devices, swap(): return lax.ppermute(block, axis, pairs)  19.3 us
    all_to_all x1, blocking collectives, body(): found = lax.all_to_all(half.reshape(pieces.shape), CHIPS, 0, 0, tiled=True)  17.2 us
    all_to_all x1, blocking collectives, collect(): half = lax.all_to_all(copies, CHIPS, 0, 0, tiled=True)  16.4 us
    all_to_all x1, waiting for transfers between devices, body(): lax.all_to_all(block, CHIPS, 0, 0, tiled=True)  11.5 us
    ppermute x3, starting transfers between devices, body(): lax.ppermute(block, 'kv', [(i, (i + 2 * (n + 1)) % heads) for i in range(...  10.5 us
    all_gather x2, blocking collectives, collect(): return lax.all_gather(half.reshape(-1, half.shape[-1]), 'core', tiled=True)  9.99 us
    all_to_all x1, starting transfers between devices, collect(): half = lax.all_to_all(copies, CHIPS, 0, 0, tiled=True)  5.53 us
  transfers between devices with their start and end apart: 8, of which 3 were waited for; matrix products, arithmetic and copies ran while one was open for 1% of the time, Pallas kernels for 1%

profile of v5, /device:TPU:1, one launch (start us, length us, event | category | flops | bytes accessed | tf_op | source)
XLA Modules:
  0.0 124.9 jit_solution(16050045675169400884)
XLA Ops:
  0.6 8.8 %collective-permute-start = (bf16[1024,256]{1,0:T(8,128)(2,1)}, bf16[1024,256]{1,0:T(8,128)(2,1)S(1)}, u32[]{:S(2)}, u32[]{:S(2)}) collective-permute-start(bf16[1024,256]{1,0:T(8,128)(2,1)} %bitcast.11), channel_id=1, source_target_pairs={{0,8},{8,0},{1,9},{9,1},{2,10},{10,2},{3,11},{11,3},{4,12},{12,4},... | collective-permute-start | bytes 1572872 | tf_op jit(solution)/shard_map/ppermute | solution.py:231
  10.7 0.1 stack.19.facts_ref
  10.8 0.3 collective-permute-done.other_ref
  11.2 1.0 copy-done
  12.2 0.6 shard_map.85
  12.8 17.2 %all_to_all.21.pieces_ref = bf16[32,16,256]{2,1,0:T(8,128)(2,1)S(1)} all-to-all(bf16[32,16,256]{2,1,0:T(8,128)(2,1)S(1)} %bitcast.10), channel_id=1, replica_groups=mesh['zl'=4,'y'=8,'core'=2,'kv'=8] {'zl','y'}, dimensions={0} | all-to-all | bytes 524288 | tf_op jit(solution)/shard_map/all_to_all | solution.py:250
  30.0 0.6 shard_map.86
  30.6 0.0 copy-start.2
  30.6 16.4 %all_to_all.22 = bf16[32,16,256]{2,1,0:T(8,128)(2,1)S(1)} all-to-all(bf16[32,16,256]{2,1,0:T(8,128)(2,1)S(1)} %shard_map.86), channel_id=1, replica_groups=mesh['zl'=4,'y'=8,'core'=2,'kv'=8] {'zl','y'}, dimensions={0} | all-to-all | bytes 524288 | tf_op jit(solution)/shard_map/all_to_all | solution.py:225
  47.0 5.3 %all_gather.6.prompt_ref = bf16[1024,256]{1,0:T(8,128)(2,1)S(1)} all-gather(bf16[512,256]{1,0:T(8,128)(2,1)S(1)} %bitcast.14), channel_id=1, replica_groups=mesh['zl'=4,'y'=8,'core'=2,'kv'=8] {'core'}, dimensions={0}, use_global_device_ids=true | all-gather | bytes 786432 | tf_op jit(solution)/shard_map/all_gather | solution.py:226
  52.3 0.0 copy-done.2
  52.3 19.8 %shard_map.87 = (f32[512,256]{1,0:T(8,128)S(1)}, bf16[512,256]{1,0:T(8,128)(2,1)S(1)}, bf16[4,32,1280]{2,1,0:T(8,128)(2,1)S(1)}, bf16[4,32,1280]{2,1,0:T(8,128)(2,1)S(1)}) custom-call(s32[5]{0:T(128)S(1)} %stack.19.facts_ref, bf16[256,1024]{1,0:T(8,128)(2,1)S(1)} %copy-done.1, bf16[256,1024]{1,0:T(8,128)(2,1)S(1)} %copy-done.2, ...), custom_call_target="tpu_custom_call" | custom-call | tf_op jit(solution)/shard_map/pallas_call | solution.py:128
  72.1 7.9 %collective-permute-start.2 = (bf16[4,32,1280]{2,1,0:T(8,128)(2,1)S(1)}, bf16[4,32,1280]{2,1,0:T(8,128)(2,1)S(1)}, u32[]{:S(2)}, u32[]{:S(2)}) collective-permute-start(bf16[4,32,1280]{2,1,0:T(8,128)(2,1)S(1)} %get-tuple-element.33), channel_id=1, source_target_pairs={{0,1},{1,0},{2,3},{3,2},{4,5},{5,4},{6,7},{7,6},{8,9},{9,8},{10,11... | collective-permute-start | bytes 983048 | tf_op jit(solution)/shard_map/ppermute | solution.py:231
  80.1 2.6 %collective-permute-start.1 = (bf16[512,256]{1,0:T(8,128)(2,1)S(1)}, bf16[512,256]{1,0:T(8,128)(2,1)S(1)}, u32[]{:S(2)}, u32[]{:S(2)}) collective-permute-start(bf16[512,256]{1,0:T(8,128)(2,1)S(1)} %get-tuple-element.30), channel_id=1, source_target_pairs={{0,8},{8,0},{1,9},{9,1},{2,10},{10,2},{3,11},{11,3},{4,12},{12,4},... | collective-permute-start | bytes 786440 | tf_op jit(solution)/shard_map/ppermute | solution.py:231
  82.7 1.1 collective-permute-done.1.other_ref
  83.8 0.7 shard_map.88
  84.6 16.1 %while.10 = (s32[]{:T(128)}, bf16[32,16,256]{2,1,0:T(8,128)(2,1)}, s32[]{:T(128)}, s32[]{:T(128)}) while((s32[]{:T(128)}, bf16[32,16,256]{2,1,0:T(8,128)(2,1)}, s32[]{:T(128)}, s32[]{:T(128)}) %tuple.20), condition=%wide.region_1.0_spmd, body=%wide.region_0.0_spmd.sunk | while | flops 2 | bytes 1310805 | solution.py:257
  84.6 3.9 %all-to-all-start = ((bf16[32,16,256]{2,1,0:T(8,128)(2,1)}), bf16[32,16,256]{2,1,0:T(8,128)(2,1)S(1)}, u32[]{:S(2)}, u32[]{:S(2)}) async-start(bf16[32,16,256]{2,1,0:T(8,128)(2,1)} %get-tuple-element.69), calls=%async_computation | async-start | bytes 524288 | tf_op jit(solution)/shard_map/while/body/all_to_all | solution.py:260
  88.4 11.5 %all-to-all-done = bf16[32,16,256]{2,1,0:T(8,128)(2,1)S(1)} async-done(((bf16[32,16,256]{2,1,0:T(8,128)(2,1)}), bf16[32,16,256]{2,1,0:T(8,128)(2,1)S(1)}, u32[]{:S(2)}, u32[]{:S(2)}) %all-to-all-start) | async-done | bytes 262176 | tf_op jit(solution)/shard_map/while/body/all_to_all | solution.py:260
  100.0 0.7 copy.14
  100.7 0.0 collective-permute-done.2.got_ref
  100.7 1.7 %shard_map.89 = (bf16[32,16,256]{2,1,0:T(8,128)(2,1)}, bf16[2,32,1280]{2,1,0:T(8,128)(2,1)S(1)}, bf16[2,32,1280]{2,1,0:T(8,128)(2,1)S(1)}, bf16[2,32,1280]{2,1,0:T(8,128)(2,1)S(1)}) custom-call(bf16[32,16,256]{2,1,0:T(8,128)(2,1)} %get-tuple-element.31.pieces_ref, bf16[4,32,1280]{2,1,0:T(8,128)(2,1)S(1)} %get-tuple-element.32.keep_ref, ...), custom_call_target="tpu_custom_call" | custom-call | tf_op jit(solution)/shard_map/pallas_call | solution.py:151
  102.4 5.5 %all-to-all-start.3 = ((bf16[32,16,256]{2,1,0:T(8,128)(2,1)}), bf16[32,16,256]{2,1,0:T(8,128)(2,1)S(1)}, u32[]{:S(2)}, u32[]{:S(2)}) async-start(bf16[32,16,256]{2,1,0:T(8,128)(2,1)} %get-tuple-element.34), calls=%async_computation.3 | async-start | bytes 524288 | tf_op jit(solution)/shard_map/all_to_all | solution.py:225
  107.9 3.1 %collective-permute-start.3 = (bf16[2,32,1280]{2,1,0:T(8,128)(2,1)S(1)}, bf16[2,32,1280]{2,1,0:T(8,128)(2,1)S(1)}, u32[]{:S(2)}, u32[]{:S(2)}) collective-permute-start(bf16[2,32,1280]{2,1,0:T(8,128)(2,1)S(1)} %get-tuple-element.35), channel_id=1, source_target_pairs={{0,2},{1,3},{2,4},{3,5},{4,6},{5,7},{6,0},{7,1},{8,10},{9,11},{10,... | collective-permute-start | bytes 491528 | tf_op jit(solution)/shard_map/ppermute | solution.py:266
  111.0 4.4 %collective-permute-start.4 = (bf16[2,32,1280]{2,1,0:T(8,128)(2,1)S(1)}, bf16[2,32,1280]{2,1,0:T(8,128)(2,1)S(1)}, u32[]{:S(2)}, u32[]{:S(2)}) collective-permute-start(bf16[2,32,1280]{2,1,0:T(8,128)(2,1)S(1)} %get-tuple-element.36), channel_id=1, source_target_pairs={{0,4},{1,5},{2,6},{3,7},{4,0},{5,1},{6,2},{7,3},{8,12},{9,13},{10,... | collective-permute-start | bytes 491528 | tf_op jit(solution)/shard_map/ppermute | solution.py:266
  115.4 3.1 %collective-permute-start.5 = (bf16[2,32,1280]{2,1,0:T(8,128)(2,1)S(1)}, bf16[2,32,1280]{2,1,0:T(8,128)(2,1)S(1)}, u32[]{:S(2)}, u32[]{:S(2)}) collective-permute-start(bf16[2,32,1280]{2,1,0:T(8,128)(2,1)S(1)} %get-tuple-element.37), channel_id=1, source_target_pairs={{0,6},{1,7},{2,0},{3,1},{4,2},{5,3},{6,4},{7,5},{8,14},{9,15},{10,... | collective-permute-start | bytes 491528 | tf_op jit(solution)/shard_map/ppermute | solution.py:266
  118.5 0.0 all-to-all-done.3
  118.5 4.7 %all_gather.7.total_ref = bf16[1024,256]{1,0:T(8,128)(2,1)S(1)} all-gather(bf16[512,256]{1,0:T(8,128)(2,1)S(1)} %bitcast.13), channel_id=1, replica_groups=mesh['zl'=4,'y'=8,'core'=2,'kv'=8] {'core'}, dimensions={0}, use_global_device_ids=true | all-gather | bytes 786432 | tf_op jit(solution)/shard_map/all_gather | solution.py:226
  123.2 0.0 collective-permute-done.3.rest_0_
  123.2 0.0 collective-permute-done.4.rest_1_
  123.2 0.0 collective-permute-done.5.rest_2_
  123.2 1.7 %shard_map.90 = (bf16[32,8192]{1,0:T(8,128)(2,1)}, bf16[32,2048]{1,0:T(8,128)(2,1)}, bf16[1,1024,256]{2,1,0:T(8,128)(2,1)}) custom-call(s32[5]{0:T(128)S(1)} %stack.19.facts_ref, bf16[1024,256]{1,0:T(8,128)(2,1)S(1)} %all_gather.7.total_ref, bf16[4,32,1280]{2,1,0:T(8,128)(2,1)S(1)} %get-tuple-element.32.keep_ref, ...), custom_call_target="tpu_custom_call" | custom-call | tf_op jit(solution)/shard_map/pallas_call | solution.py:151
  (5 shorter events, 0.0 us)
Async XLA Ops:
  0.6 10.5 %collective-permute-start = (bf16[1024,256]{1,0:T(8,128)(2,1)}, bf16[1024,256]{1,0:T(8,128)(2,1)S(1)}, u32[]{:S(2)}, u32[]{:S(2)}) collective-permute-start(bf16[1024,256]{1,0:T(8,128)(2,1)} %bitcast.11), channel_id=1, source_target_pairs={{0,8},{8,0},{1,9},{9,1},{2,10},{10,2},{3,11},{11,3},{4,12},{12,4},... | collective-permute-start | bytes 1572872 | tf_op jit(solution)/shard_map/ppermute | solution.py:231
  11.2 1.0 copy-start
  30.6 21.7 %copy-start.2 = (bf16[256,1024]{1,0:T(8,128)(2,1)S(1)}, bf16[256,1024]{1,0:T(8,128)(2,1)}, u32[]{:S(2)}) copy-start(bf16[256,1024]{1,0:T(8,128)(2,1)} %grad_ref.1) | copy-start | bytes 1572868
  47.0 5.3 %copy-start.1 = (bf16[256,1024]{1,0:T(8,128)(2,1)S(1)}, bf16[256,1024]{1,0:T(8,128)(2,1)}, u32[]{:S(2)}) copy-start(bf16[256,1024]{1,0:T(8,128)(2,1)} %query_ref.1) | copy-start | bytes 1572868
  47.0 5.3 %copy-start.3 = (bf16[256,256]{1,0:T(8,128)(2,1)S(1)}, bf16[256,256]{1,0:T(8,128)(2,1)}, u32[]{:S(2)}) copy-start(bf16[256,256]{1,0:T(8,128)(2,1)} %cont_ref.1) | copy-start | bytes 393220
  72.1 28.5 %collective-permute-start.2 = (bf16[4,32,1280]{2,1,0:T(8,128)(2,1)S(1)}, bf16[4,32,1280]{2,1,0:T(8,128)(2,1)S(1)}, u32[]{:S(2)}, u32[]{:S(2)}) collective-permute-start(bf16[4,32,1280]{2,1,0:T(8,128)(2,1)S(1)} %get-tuple-element.33), channel_id=1, source_target_pairs={{0,1},{1,0},{2,3},{3,2},{4,5},{5,4},{6,7},{7,6},{8,9},{9,8},{10,11... | collective-permute-start | bytes 983048 | tf_op jit(solution)/shard_map/ppermute | solution.py:231
  80.1 3.7 %collective-permute-start.1 = (bf16[512,256]{1,0:T(8,128)(2,1)S(1)}, bf16[512,256]{1,0:T(8,128)(2,1)S(1)}, u32[]{:S(2)}, u32[]{:S(2)}) collective-permute-start(bf16[512,256]{1,0:T(8,128)(2,1)S(1)} %get-tuple-element.30), channel_id=1, source_target_pairs={{0,8},{8,0},{1,9},{9,1},{2,10},{10,2},{3,11},{11,3},{4,12},{12,4},... | collective-permute-start | bytes 786440 | tf_op jit(solution)/shard_map/ppermute | solution.py:231
  84.6 15.4 %all-to-all-start = ((bf16[32,16,256]{2,1,0:T(8,128)(2,1)}), bf16[32,16,256]{2,1,0:T(8,128)(2,1)S(1)}, u32[]{:S(2)}, u32[]{:S(2)}) async-start(bf16[32,16,256]{2,1,0:T(8,128)(2,1)} %get-tuple-element.69), calls=%async_computation | async-start | bytes 524288 | tf_op jit(solution)/shard_map/while/body/all_to_all | solution.py:260
  102.4 16.1 %all-to-all-start.3 = ((bf16[32,16,256]{2,1,0:T(8,128)(2,1)}), bf16[32,16,256]{2,1,0:T(8,128)(2,1)S(1)}, u32[]{:S(2)}, u32[]{:S(2)}) async-start(bf16[32,16,256]{2,1,0:T(8,128)(2,1)} %get-tuple-element.34), calls=%async_computation.3 | async-start | bytes 524288 | tf_op jit(solution)/shard_map/all_to_all | solution.py:225
  107.9 15.3 %collective-permute-start.3 = (bf16[2,32,1280]{2,1,0:T(8,128)(2,1)S(1)}, bf16[2,32,1280]{2,1,0:T(8,128)(2,1)S(1)}, u32[]{:S(2)}, u32[]{:S(2)}) collective-permute-start(bf16[2,32,1280]{2,1,0:T(8,128)(2,1)S(1)} %get-tuple-element.35), channel_id=1, source_target_pairs={{0,2},{1,3},{2,4},{3,5},{4,6},{5,7},{6,0},{7,1},{8,10},{9,11},{10,... | collective-permute-start | bytes 491528 | tf_op jit(solution)/shard_map/ppermute | solution.py:266
  111.0 12.2 %collective-permute-start.4 = (bf16[2,32,1280]{2,1,0:T(8,128)(2,1)S(1)}, bf16[2,32,1280]{2,1,0:T(8,128)(2,1)S(1)}, u32[]{:S(2)}, u32[]{:S(2)}) collective-permute-start(bf16[2,32,1280]{2,1,0:T(8,128)(2,1)S(1)} %get-tuple-element.36), channel_id=1, source_target_pairs={{0,4},{1,5},{2,6},{3,7},{4,0},{5,1},{6,2},{7,3},{8,12},{9,13},{10,... | collective-permute-start | bytes 491528 | tf_op jit(solution)/shard_map/ppermute | solution.py:266
  115.4 7.8 %collective-permute-start.5 = (bf16[2,32,1280]{2,1,0:T(8,128)(2,1)S(1)}, bf16[2,32,1280]{2,1,0:T(8,128)(2,1)S(1)}, u32[]{:S(2)}, u32[]{:S(2)}) collective-permute-start(bf16[2,32,1280]{2,1,0:T(8,128)(2,1)S(1)} %get-tuple-element.37), channel_id=1, source_target_pairs={{0,6},{1,7},{2,0},{3,1},{4,2},{5,3},{6,4},{7,5},{8,14},{9,15},{10,... | collective-permute-start | bytes 491528 | tf_op jit(solution)/shard_map/ppermute | solution.py:266

commit v6 on v5

--- a/solution.py
+++ b/solution.py
@@ -252,12 +252,13 @@
     shared = collect(copies)
 
     own, other, keep, give = attention_grads(query, out_grad, shared, cont_kv, facts, ring)
+    other = swap(other, "core")
     got = swap(give, "kv")
-    parts = local_call(add_halves, pieces, own, swap(other, "core"))
-    parts = lax.fori_loop(
-        0,
-        jnp.minimum(lengths[0], 1),
-        lambda _, block: lax.all_to_all(block, CHIPS, 0, 0, tiled=True),
+    parts = local_call(add_halves, pieces, own, other)
+    parts = lax.cond(
+        lengths[0] > 0,
+        lambda block: lax.all_to_all(block, CHIPS, 0, 0, tiled=True),
+        lambda block: block,
         parts,
     )
     send = like((2, *keep.shape[1:]))

time: 125 us -> 124 us (level)
  blocking collectives: 43.6 us -> 58.5 us
  waiting for transfers between devices: 13 us -> 1.49 us
  starting transfers between devices: 39.2 us -> 36.5 us
  Pallas kernels: 25.1 us -> 23.5 us
    all_to_all x0 -> x1, blocking collectives: none -> 14.9 us  [body(): lax.all_to_all(block, CHIPS, 0, 0, tiled=True)]
    all_to_all x1 -> x0, waiting for transfers between devices: 11.5 us -> none  [body(): lax.all_to_all(block, CHIPS, 0, 0, tiled=True)]
    all_to_all x1 -> x0, starting transfers between devices: 3.87 us -> none  [body(): lax.all_to_all(block, CHIPS, 0, 0, tiled=True)]
    pallas_call x5, Pallas kernels: 5.28 us -> 3.63 us  [local_call(): pl.pallas_call(kernel, out_shape=outs, in_specs=places or [VMEM] * len(ar...]
  transfers between devices with their start and end apart: 8 -> 7, of which waited for: 3 -> 2; matrix products, arithmetic and copies ran while one was open for 1% -> 0% of each run, Pallas kernels for 1% -> 0%
where the time goes in v6:
time: 124 us; the launch traced here: 123 us
  blocking collectives  58.5 us (47%)
  starting transfers between devices  36.5 us (29%)
  Pallas kernels  23.5 us (19%)
  between operations  2.05 us (2%)
  waiting for transfers between devices  1.49 us (1%)
    pallas_call x1, Pallas kernels, attention_grads(): pl.pallas_call(attention_kernel, out_shape=(like((prompt_len // 2, both),...  19.8 us
    ppermute x3, starting transfers between devices, swap(): return lax.ppermute(block, axis, pairs)  19.3 us
    all_to_all x1, blocking collectives, body(): found = lax.all_to_all(half.reshape(pieces.shape), CHIPS, 0, 0, tiled=True)  17.2 us
    all_to_all x1, blocking collectives, collect(): half = lax.all_to_all(copies, CHIPS, 0, 0, tiled=True)  16.4 us
    all_to_all x1, blocking collectives, body(): lax.all_to_all(block, CHIPS, 0, 0, tiled=True)  14.9 us
    ppermute x3, starting transfers between devices, body(): lax.ppermute(block, 'kv', [(i, (i + 2 * (n + 1)) % heads) for i in range(...  10.5 us
    all_gather x2, blocking collectives, collect(): return lax.all_gather(half.reshape(-1, half.shape[-1]), 'core', tiled=True)  9.98 us
    all_to_all x1, starting transfers between devices, collect(): half = lax.all_to_all(copies, CHIPS, 0, 0, tiled=True)  6.69 us
  transfers between devices with their start and end apart: 7, of which 2 were waited for; matrix products, arithmetic and copies ran while one was open for 0% of the time, Pallas kernels for 0%

profile of v6, /device:TPU:1, one launch (start us, length us, event | category | flops | bytes accessed | tf_op | source)
XLA Modules:
  0.0 123.2 jit_solution(5535433740977024762)
XLA Ops:
  0.6 8.8 %collective-permute-start = (bf16[1024,256]{1,0:T(8,128)(2,1)}, bf16[1024,256]{1,0:T(8,128)(2,1)S(1)}, u32[]{:S(2)}, u32[]{:S(2)}) collective-permute-start(bf16[1024,256]{1,0:T(8,128)(2,1)} %bitcast.11), channel_id=1, source_target_pairs={{0,8},{8,0},{1,9},{9,1},{2,10},{10,2},{3,11},{11,3},{4,12},{12,4},... | collective-permute-start | bytes 1572872 | tf_op jit(solution)/shard_map/ppermute | solution.py:231
  10.7 0.1 stack.19.facts_ref
  10.8 0.3 collective-permute-done.other_ref
  11.2 0.0 copy-start
  11.2 1.0 copy-done
  12.2 0.6 shard_map.85
  12.8 17.2 %all_to_all.20.pieces_ref = bf16[32,16,256]{2,1,0:T(8,128)(2,1)S(1)} all-to-all(bf16[32,16,256]{2,1,0:T(8,128)(2,1)S(1)} %bitcast.10), channel_id=1, replica_groups=mesh['zl'=4,'y'=8,'core'=2,'kv'=8] {'zl','y'}, dimensions={0} | all-to-all | bytes 524288 | tf_op jit(solution)/shard_map/all_to_all | solution.py:250
  30.0 0.6 shard_map.86
  30.6 0.0 copy-start.2
  30.6 16.4 %all_to_all.21 = bf16[32,16,256]{2,1,0:T(8,128)(2,1)S(1)} all-to-all(bf16[32,16,256]{2,1,0:T(8,128)(2,1)S(1)} %shard_map.86), channel_id=1, replica_groups=mesh['zl'=4,'y'=8,'core'=2,'kv'=8] {'zl','y'}, dimensions={0} | all-to-all | bytes 524288 | tf_op jit(solution)/shard_map/all_to_all | solution.py:225
  47.0 5.3 %all_gather.6.prompt_ref = bf16[1024,256]{1,0:T(8,128)(2,1)S(1)} all-gather(bf16[512,256]{1,0:T(8,128)(2,1)S(1)} %bitcast.14), channel_id=1, replica_groups=mesh['zl'=4,'y'=8,'core'=2,'kv'=8] {'core'}, dimensions={0}, use_global_device_ids=true | all-gather | bytes 786432 | tf_op jit(solution)/shard_map/all_gather | solution.py:226
  52.3 0.0 copy-done.2
  52.3 0.0 copy-done.1
  52.3 0.0 copy-done.3
  52.3 19.8 %shard_map.87 = (f32[512,256]{1,0:T(8,128)S(1)}, bf16[512,256]{1,0:T(8,128)(2,1)S(1)}, bf16[4,32,1280]{2,1,0:T(8,128)(2,1)S(1)}, bf16[4,32,1280]{2,1,0:T(8,128)(2,1)S(1)}) custom-call(s32[5]{0:T(128)S(1)} %stack.19.facts_ref, bf16[256,1024]{1,0:T(8,128)(2,1)S(1)} %copy-done.1, bf16[256,1024]{1,0:T(8,128)(2,1)S(1)} %copy-done.2, ...), custom_call_target="tpu_custom_call" | custom-call | tf_op jit(solution)/shard_map/pallas_call | solution.py:128
  72.1 7.9 %collective-permute-start.2 = (bf16[4,32,1280]{2,1,0:T(8,128)(2,1)S(1)}, bf16[4,32,1280]{2,1,0:T(8,128)(2,1)S(1)}, u32[]{:S(2)}, u32[]{:S(2)}) collective-permute-start(bf16[4,32,1280]{2,1,0:T(8,128)(2,1)S(1)} %get-tuple-element.19), channel_id=1, source_target_pairs={{0,1},{1,0},{2,3},{3,2},{4,5},{5,4},{6,7},{7,6},{8,9},{9,8},{10,11... | collective-permute-start | bytes 983048 | tf_op jit(solution)/shard_map/ppermute | solution.py:231
  80.1 2.6 %collective-permute-start.1 = (bf16[512,256]{1,0:T(8,128)(2,1)S(1)}, bf16[512,256]{1,0:T(8,128)(2,1)S(1)}, u32[]{:S(2)}, u32[]{:S(2)}) collective-permute-start(bf16[512,256]{1,0:T(8,128)(2,1)S(1)} %get-tuple-element.17), channel_id=1, source_target_pairs={{0,8},{8,0},{1,9},{9,1},{2,10},{10,2},{3,11},{11,3},{4,12},{12,4},... | collective-permute-start | bytes 786440 | tf_op jit(solution)/shard_map/ppermute | solution.py:231
  82.7 1.1 collective-permute-done.1.other_ref
  83.8 15.0 %conditional.1 = (bf16[32,16,256]{2,1,0:T(8,128)(2,1)S(1)}) conditional(s32[]{:T(128)} %bitcast.4, bf16[32,16,256]{2,1,0:T(8,128)(2,1)S(1)} %shard_map.88, bf16[32,16,256]{2,1,0:T(8,128)(2,1)S(1)} %shard_map.88), branch_computations={%region_0.0_spmd, %region_1.0_spmd} | conditional | bytes 1048584 | solution.py:258
  83.9 14.9 %all_to_all.19 = bf16[32,16,256]{2,1,0:T(8,128)(2,1)S(1)} all-to-all(bf16[32,16,256]{2,1,0:T(8,128)(2,1)S(1)} %copy.13), channel_id=1, replica_groups=mesh['zl'=4,'y'=8,'core'=2,'kv'=8] {'zl','y'}, dimensions={0} | all-to-all | bytes 524288 | tf_op jit(solution)/shard_map/cond/branch_1_fun/all_to_all | solution.py:260
  98.8 0.0 collective-permute-done.2.got_ref
  98.8 0.8 shard_map.89
  99.6 6.7 %all-to-all-start.3 = ((bf16[32,16,256]{2,1,0:T(8,128)(2,1)}), bf16[32,16,256]{2,1,0:T(8,128)(2,1)S(1)}, u32[]{:S(2)}, u32[]{:S(2)}) async-start(bf16[32,16,256]{2,1,0:T(8,128)(2,1)} %get-tuple-element.20), calls=%async_computation.3 | async-start | bytes 524288 | tf_op jit(solution)/shard_map/all_to_all | solution.py:225
  106.3 3.1 %collective-permute-start.3 = (bf16[2,32,1280]{2,1,0:T(8,128)(2,1)S(1)}, bf16[2,32,1280]{2,1,0:T(8,128)(2,1)S(1)}, u32[]{:S(2)}, u32[]{:S(2)}) collective-permute-start(bf16[2,32,1280]{2,1,0:T(8,128)(2,1)S(1)} %get-tuple-element.21), channel_id=1, source_target_pairs={{0,2},{1,3},{2,4},{3,5},{4,6},{5,7},{6,0},{7,1},{8,10},{9,11},{10,... | collective-permute-start | bytes 491528 | tf_op jit(solution)/shard_map/ppermute | solution.py:267
  109.4 4.4 %collective-permute-start.4 = (bf16[2,32,1280]{2,1,0:T(8,128)(2,1)S(1)}, bf16[2,32,1280]{2,1,0:T(8,128)(2,1)S(1)}, u32[]{:S(2)}, u32[]{:S(2)}) collective-permute-start(bf16[2,32,1280]{2,1,0:T(8,128)(2,1)S(1)} %get-tuple-element.22), channel_id=1, source_target_pairs={{0,4},{1,5},{2,6},{3,7},{4,0},{5,1},{6,2},{7,3},{8,12},{9,13},{10,... | collective-permute-start | bytes 491528 | tf_op jit(solution)/shard_map/ppermute | solution.py:267
  113.8 3.1 %collective-permute-start.5 = (bf16[2,32,1280]{2,1,0:T(8,128)(2,1)S(1)}, bf16[2,32,1280]{2,1,0:T(8,128)(2,1)S(1)}, u32[]{:S(2)}, u32[]{:S(2)}) collective-permute-start(bf16[2,32,1280]{2,1,0:T(8,128)(2,1)S(1)} %get-tuple-element.23), channel_id=1, source_target_pairs={{0,6},{1,7},{2,0},{3,1},{4,2},{5,3},{6,4},{7,5},{8,14},{9,15},{10,... | collective-permute-start | bytes 491528 | tf_op jit(solution)/shard_map/ppermute | solution.py:267
  116.9 0.0 all-to-all-done.3
  116.9 4.7 %all_gather.7.total_ref = bf16[1024,256]{1,0:T(8,128)(2,1)S(1)} all-gather(bf16[512,256]{1,0:T(8,128)(2,1)S(1)} %bitcast.13), channel_id=1, replica_groups=mesh['zl'=4,'y'=8,'core'=2,'kv'=8] {'core'}, dimensions={0}, use_global_device_ids=true | all-gather | bytes 786432 | tf_op jit(solution)/shard_map/all_gather | solution.py:226
  121.6 0.0 collective-permute-done.3.rest_0_
  121.6 0.0 collective-permute-done.4.rest_1_
  121.6 0.0 collective-permute-done.5.rest_2_
  121.6 1.7 %shard_map.90 = (bf16[32,8192]{1,0:T(8,128)(2,1)}, bf16[32,2048]{1,0:T(8,128)(2,1)}, bf16[1,1024,256]{2,1,0:T(8,128)(2,1)}) custom-call(s32[5]{0:T(128)S(1)} %stack.19.facts_ref, bf16[1024,256]{1,0:T(8,128)(2,1)S(1)} %all_gather.7.total_ref, bf16[4,32,1280]{2,1,0:T(8,128)(2,1)S(1)} %get-tuple-element.18.keep_ref, ...), custom_call_target="tpu_custom_call" | custom-call | tf_op jit(solution)/shard_map/pallas_call | solution.py:151
  (4 shorter events, 0.1 us)
Async XLA Ops:
  0.6 10.5 %collective-permute-start = (bf16[1024,256]{1,0:T(8,128)(2,1)}, bf16[1024,256]{1,0:T(8,128)(2,1)S(1)}, u32[]{:S(2)}, u32[]{:S(2)}) collective-permute-start(bf16[1024,256]{1,0:T(8,128)(2,1)} %bitcast.11), channel_id=1, source_target_pairs={{0,8},{8,0},{1,9},{9,1},{2,10},{10,2},{3,11},{11,3},{4,12},{12,4},... | collective-permute-start | bytes 1572872 | tf_op jit(solution)/shard_map/ppermute | solution.py:231
  11.2 1.0 copy-start
  30.6 21.7 %copy-start.2 = (bf16[256,1024]{1,0:T(8,128)(2,1)S(1)}, bf16[256,1024]{1,0:T(8,128)(2,1)}, u32[]{:S(2)}) copy-start(bf16[256,1024]{1,0:T(8,128)(2,1)} %grad_ref.1) | copy-start | bytes 1572868
  47.0 5.3 %copy-start.1 = (bf16[256,1024]{1,0:T(8,128)(2,1)S(1)}, bf16[256,1024]{1,0:T(8,128)(2,1)}, u32[]{:S(2)}) copy-start(bf16[256,1024]{1,0:T(8,128)(2,1)} %query_ref.1) | copy-start | bytes 1572868
  47.0 5.3 %copy-start.3 = (bf16[256,256]{1,0:T(8,128)(2,1)S(1)}, bf16[256,256]{1,0:T(8,128)(2,1)}, u32[]{:S(2)}) copy-start(bf16[256,256]{1,0:T(8,128)(2,1)} %cont_ref.1) | copy-start | bytes 393220
  72.1 26.7 %collective-permute-start.2 = (bf16[4,32,1280]{2,1,0:T(8,128)(2,1)S(1)}, bf16[4,32,1280]{2,1,0:T(8,128)(2,1)S(1)}, u32[]{:S(2)}, u32[]{:S(2)}) collective-permute-start(bf16[4,32,1280]{2,1,0:T(8,128)(2,1)S(1)} %get-tuple-element.19), channel_id=1, source_target_pairs={{0,1},{1,0},{2,3},{3,2},{4,5},{5,4},{6,7},{7,6},{8,9},{9,8},{10,11... | collective-permute-start | bytes 983048 | tf_op jit(solution)/shard_map/ppermute | solution.py:231
  80.1 3.7 %collective-permute-start.1 = (bf16[512,256]{1,0:T(8,128)(2,1)S(1)}, bf16[512,256]{1,0:T(8,128)(2,1)S(1)}, u32[]{:S(2)}, u32[]{:S(2)}) collective-permute-start(bf16[512,256]{1,0:T(8,128)(2,1)S(1)} %get-tuple-element.17), channel_id=1, source_target_pairs={{0,8},{8,0},{1,9},{9,1},{2,10},{10,2},{3,11},{11,3},{4,12},{12,4},... | collective-permute-start | bytes 786440 | tf_op jit(solution)/shard_map/ppermute | solution.py:231
  99.6 17.3 %all-to-all-start.3 = ((bf16[32,16,256]{2,1,0:T(8,128)(2,1)}), bf16[32,16,256]{2,1,0:T(8,128)(2,1)S(1)}, u32[]{:S(2)}, u32[]{:S(2)}) async-start(bf16[32,16,256]{2,1,0:T(8,128)(2,1)} %get-tuple-element.20), calls=%async_computation.3 | async-start | bytes 524288 | tf_op jit(solution)/shard_map/all_to_all | solution.py:225
  106.3 15.3 %collective-permute-start.3 = (bf16[2,32,1280]{2,1,0:T(8,128)(2,1)S(1)}, bf16[2,32,1280]{2,1,0:T(8,128)(2,1)S(1)}, u32[]{:S(2)}, u32[]{:S(2)}) collective-permute-start(bf16[2,32,1280]{2,1,0:T(8,128)(2,1)S(1)} %get-tuple-element.21), channel_id=1, source_target_pairs={{0,2},{1,3},{2,4},{3,5},{4,6},{5,7},{6,0},{7,1},{8,10},{9,11},{10,... | collective-permute-start | bytes 491528 | tf_op jit(solution)/shard_map/ppermute | solution.py:267
  109.4 12.1 %collective-permute-start.4 = (bf16[2,32,1280]{2,1,0:T(8,128)(2,1)S(1)}, bf16[2,32,1280]{2,1,0:T(8,128)(2,1)S(1)}, u32[]{:S(2)}, u32[]{:S(2)}) collective-permute-start(bf16[2,32,1280]{2,1,0:T(8,128)(2,1)S(1)} %get-tuple-element.22), channel_id=1, source_target_pairs={{0,4},{1,5},{2,6},{3,7},{4,0},{5,1},{6,2},{7,3},{8,12},{9,13},{10,... | collective-permute-start | bytes 491528 | tf_op jit(solution)/shard_map/ppermute | solution.py:267
  113.8 7.8 %collective-permute-start.5 = (bf16[2,32,1280]{2,1,0:T(8,128)(2,1)S(1)}, bf16[2,32,1280]{2,1,0:T(8,128)(2,1)S(1)}, u32[]{:S(2)}, u32[]{:S(2)}) collective-permute-start(bf16[2,32,1280]{2,1,0:T(8,128)(2,1)S(1)} %get-tuple-element.23), channel_id=1, source_target_pairs={{0,6},{1,7},{2,0},{3,1},{4,2},{5,3},{6,4},{7,5},{8,14},{9,15},{10,... | collective-permute-start | bytes 491528 | tf_op jit(solution)/shard_map/ppermute | solution.py:267

commit v7 on v6

--- a/solution.py
+++ b/solution.py
@@ -180,8 +180,8 @@
         copies_ref[peer] = piece
 
 
-def add_halves(own_ref, other_ref, pieces_ref):
-    half = own_ref[...] + other_ref[...].astype(jnp.float32)
+def add_halves(facts_ref, own_ref, others_ref, pieces_ref):
+    half = own_ref[...] + others_ref[1 - facts_ref[CORE]].astype(jnp.float32)
     pieces_ref[...] = half.astype(jnp.bfloat16).reshape(pieces_ref.shape)
 
 
@@ -252,9 +252,9 @@
     shared = collect(copies)
 
     own, other, keep, give = attention_grads(query, out_grad, shared, cont_kv, facts, ring)
-    other = swap(other, "core")
     got = swap(give, "kv")
-    parts = local_call(add_halves, pieces, own, other)
+    others = lax.all_gather(other, "core")
+    parts = local_call(add_halves, pieces, facts, own, others, places=[SMEM, VMEM, VMEM])
     parts = lax.cond(
         lengths[0] > 0,
         lambda block: lax.all_to_all(block, CHIPS, 0, 0, tiled=True),

time: 124 us -> 124 us (level)
  blocking collectives: 58.5 us -> 61.8 us
  starting transfers between devices: 36.5 us -> 33.8 us
    ppermute x3 -> x2, starting transfers between devices: 19.3 us -> 16.7 us  [swap(): return lax.ppermute(block, axis, pairs)]
    all_gather x0 -> x1, blocking collectives: none -> 2.47 us  [body(): others = lax.all_gather(other, 'core')]
  transfers between devices with their start and end apart: 7 -> 6, of which waited for: 2 -> 1; matrix products, arithmetic and copies ran while one was open for 0% -> 0% of each run, Pallas kernels for 0% -> 0%
where the time goes in v7:
time: 124 us; the launch traced here: 123 us
  blocking collectives  61.8 us (50%)
  starting transfers between devices  33.8 us (27%)
  Pallas kernels  24 us (19%)
  between operations  2.05 us (2%)
    pallas_call x1, Pallas kernels, attention_grads(): pl.pallas_call(attention_kernel, out_shape=(like((prompt_len // 2, both),...  19.8 us
    all_to_all x1, blocking collectives, body(): found = lax.all_to_all(half.reshape(pieces.shape), CHIPS, 0, 0, tiled=True)  17.2 us
    ppermute x2, starting transfers between devices, swap(): return lax.ppermute(block, axis, pairs)  16.7 us
    all_to_all x1, blocking collectives, collect(): half = lax.all_to_all(copies, CHIPS, 0, 0, tiled=True)  16.4 us
    all_to_all x1, blocking collectives, body(): lax.all_to_all(block, CHIPS, 0, 0, tiled=True)  15.7 us
    ppermute x3, starting transfers between devices, body(): lax.ppermute(block, 'kv', [(i, (i + 2 * (n + 1)) % heads) for i in range(...  10.5 us
    all_gather x2, blocking collectives, collect(): return lax.all_gather(half.reshape(-1, half.shape[-1]), 'core', tiled=True)  9.99 us
    all_to_all x1, starting transfers between devices, collect(): half = lax.all_to_all(copies, CHIPS, 0, 0, tiled=True)  6.54 us
  transfers between devices with their start and end apart: 6, of which 1 were waited for; matrix products, arithmetic and copies ran while one was open for 0% of the time, Pallas kernels for 0%

profile of v7, /device:TPU:1, one launch (start us, length us, event | category | flops | bytes accessed | tf_op | source)
XLA Modules:
  0.0 123.2 jit_solution(1446415349635887560)
XLA Ops:
  0.6 8.8 %collective-permute-start = (bf16[1024,256]{1,0:T(8,128)(2,1)}, bf16[1024,256]{1,0:T(8,128)(2,1)S(1)}, u32[]{:S(2)}, u32[]{:S(2)}) collective-permute-start(bf16[1024,256]{1,0:T(8,128)(2,1)} %bitcast.13), channel_id=1, source_target_pairs={{0,8},{8,0},{1,9},{9,1},{2,10},{10,2},{3,11},{11,3},{4,12},{12,4},... | collective-permute-start | bytes 1572872 | tf_op jit(solution)/shard_map/ppermute | solution.py:231
  10.7 0.1 stack.19.facts_ref
  10.8 0.3 collective-permute-done.other_ref
  11.2 0.0 copy-start
  11.2 1.0 copy-done
  12.2 0.6 shard_map.85
  12.8 17.2 %all_to_all.20.pieces_ref = bf16[32,16,256]{2,1,0:T(8,128)(2,1)S(1)} all-to-all(bf16[32,16,256]{2,1,0:T(8,128)(2,1)S(1)} %bitcast.12), channel_id=1, replica_groups=mesh['zl'=4,'y'=8,'core'=2,'kv'=8] {'zl','y'}, dimensions={0} | all-to-all | bytes 524288 | tf_op jit(solution)/shard_map/all_to_all | solution.py:250
  30.0 0.6 shard_map.86
  30.6 0.0 copy-start.2
  30.6 16.4 %all_to_all.21 = bf16[32,16,256]{2,1,0:T(8,128)(2,1)S(1)} all-to-all(bf16[32,16,256]{2,1,0:T(8,128)(2,1)S(1)} %shard_map.86), channel_id=1, replica_groups=mesh['zl'=4,'y'=8,'core'=2,'kv'=8] {'zl','y'}, dimensions={0} | all-to-all | bytes 524288 | tf_op jit(solution)/shard_map/all_to_all | solution.py:225
  47.0 5.3 %all_gather.12.prompt_ref = bf16[1024,256]{1,0:T(8,128)(2,1)S(1)} all-gather(bf16[512,256]{1,0:T(8,128)(2,1)S(1)} %bitcast.16), channel_id=1, replica_groups=mesh['zl'=4,'y'=8,'core'=2,'kv'=8] {'core'}, dimensions={0}, use_global_device_ids=true | all-gather | bytes 786432 | tf_op jit(solution)/shard_map/all_gather | solution.py:226
  52.3 0.0 copy-done.2
  52.3 0.0 copy-done.1
  52.3 0.0 copy-done.3
  52.3 19.8 %shard_map.87 = (f32[512,256]{1,0:T(8,128)S(1)}, bf16[512,256]{1,0:T(8,128)(2,1)S(1)}, bf16[4,32,1280]{2,1,0:T(8,128)(2,1)S(1)}, bf16[4,32,1280]{2,1,0:T(8,128)(2,1)S(1)}) custom-call(s32[5]{0:T(128)S(1)} %stack.19.facts_ref, bf16[256,1024]{1,0:T(8,128)(2,1)S(1)} %copy-done.1, bf16[256,1024]{1,0:T(8,128)(2,1)S(1)} %copy-done.2, ...), custom_call_target="tpu_custom_call" | custom-call | tf_op jit(solution)/shard_map/pallas_call | solution.py:128
  72.1 7.9 %collective-permute-start.1 = (bf16[4,32,1280]{2,1,0:T(8,128)(2,1)S(1)}, bf16[4,32,1280]{2,1,0:T(8,128)(2,1)S(1)}, u32[]{:S(2)}, u32[]{:S(2)}) collective-permute-start(bf16[4,32,1280]{2,1,0:T(8,128)(2,1)S(1)} %get-tuple-element.19), channel_id=1, source_target_pairs={{0,1},{1,0},{2,3},{3,2},{4,5},{5,4},{6,7},{7,6},{8,9},{9,8},{10,11... | collective-permute-start | bytes 983048 | tf_op jit(solution)/shard_map/ppermute | solution.py:231
  80.1 2.5 %all-gather = bf16[1024,256]{1,0:T(8,128)(2,1)S(1)} all-gather(bf16[512,256]{1,0:T(8,128)(2,1)S(1)} %get-tuple-element.17), channel_id=2, replica_groups=mesh['zl'=4,'y'=8,'core'=2,'kv'=8] {'core'}, dimensions={0}, use_global_device_ids=true | all-gather | bytes 786432 | tf_op jit(solution)/shard_map/all_gather | solution.py:256
  82.6 0.6 shard_map.88
  83.2 15.8 %conditional.1 = (bf16[32,16,256]{2,1,0:T(8,128)(2,1)S(1)}) conditional(s32[]{:T(128)} %bitcast.4, bf16[32,16,256]{2,1,0:T(8,128)(2,1)S(1)} %shard_map.88, bf16[32,16,256]{2,1,0:T(8,128)(2,1)S(1)} %shard_map.88), branch_computations={%region_0.0_spmd, %region_1.0_spmd} | conditional | bytes 1048584 | solution.py:258
  83.2 15.7 %all_to_all.19 = bf16[32,16,256]{2,1,0:T(8,128)(2,1)S(1)} all-to-all(bf16[32,16,256]{2,1,0:T(8,128)(2,1)S(1)} %copy.13), channel_id=1, replica_groups=mesh['zl'=4,'y'=8,'core'=2,'kv'=8] {'zl','y'}, dimensions={0} | all-to-all | bytes 524288 | tf_op jit(solution)/shard_map/cond/branch_1_fun/all_to_all | solution.py:260
  99.0 0.0 collective-permute-done.1.got_ref
  99.0 0.8 shard_map.89
  99.7 6.5 %all-to-all-start.3 = ((bf16[32,16,256]{2,1,0:T(8,128)(2,1)}), bf16[32,16,256]{2,1,0:T(8,128)(2,1)S(1)}, u32[]{:S(2)}, u32[]{:S(2)}) async-start(bf16[32,16,256]{2,1,0:T(8,128)(2,1)} %get-tuple-element.20), calls=%async_computation.3 | async-start | bytes 524288 | tf_op jit(solution)/shard_map/all_to_all | solution.py:225
  106.3 3.1 %collective-permute-start.2 = (bf16[2,32,1280]{2,1,0:T(8,128)(2,1)S(1)}, bf16[2,32,1280]{2,1,0:T(8,128)(2,1)S(1)}, u32[]{:S(2)}, u32[]{:S(2)}) collective-permute-start(bf16[2,32,1280]{2,1,0:T(8,128)(2,1)S(1)} %get-tuple-element.21), channel_id=1, source_target_pairs={{0,2},{1,3},{2,4},{3,5},{4,6},{5,7},{6,0},{7,1},{8,10},{9,11},{10,... | collective-permute-start | bytes 491528 | tf_op jit(solution)/shard_map/ppermute | solution.py:267
  109.4 4.4 %collective-permute-start.3 = (bf16[2,32,1280]{2,1,0:T(8,128)(2,1)S(1)}, bf16[2,32,1280]{2,1,0:T(8,128)(2,1)S(1)}, u32[]{:S(2)}, u32[]{:S(2)}) collective-permute-start(bf16[2,32,1280]{2,1,0:T(8,128)(2,1)S(1)} %get-tuple-element.22), channel_id=1, source_target_pairs={{0,4},{1,5},{2,6},{3,7},{4,0},{5,1},{6,2},{7,3},{8,12},{9,13},{10,... | collective-permute-start | bytes 491528 | tf_op jit(solution)/shard_map/ppermute | solution.py:267
  113.8 3.1 %collective-permute-start.4 = (bf16[2,32,1280]{2,1,0:T(8,128)(2,1)S(1)}, bf16[2,32,1280]{2,1,0:T(8,128)(2,1)S(1)}, u32[]{:S(2)}, u32[]{:S(2)}) collective-permute-start(bf16[2,32,1280]{2,1,0:T(8,128)(2,1)S(1)} %get-tuple-element.23), channel_id=1, source_target_pairs={{0,6},{1,7},{2,0},{3,1},{4,2},{5,3},{6,4},{7,5},{8,14},{9,15},{10,... | collective-permute-start | bytes 491528 | tf_op jit(solution)/shard_map/ppermute | solution.py:267
  116.9 0.0 all-to-all-done.3
  116.9 4.7 %all_gather.15.total_ref = bf16[1024,256]{1,0:T(8,128)(2,1)S(1)} all-gather(bf16[512,256]{1,0:T(8,128)(2,1)S(1)} %bitcast.15), channel_id=1, replica_groups=mesh['zl'=4,'y'=8,'core'=2,'kv'=8] {'core'}, dimensions={0}, use_global_device_ids=true | all-gather | bytes 786432 | tf_op jit(solution)/shard_map/all_gather | solution.py:226
  121.6 0.0 collective-permute-done.2.rest_0_
  121.6 0.0 collective-permute-done.3.rest_1_
  121.6 0.0 collective-permute-done.4.rest_2_
  121.6 1.7 %shard_map.90 = (bf16[32,8192]{1,0:T(8,128)(2,1)}, bf16[32,2048]{1,0:T(8,128)(2,1)}, bf16[1,1024,256]{2,1,0:T(8,128)(2,1)}) custom-call(s32[5]{0:T(128)S(1)} %stack.19.facts_ref, bf16[1024,256]{1,0:T(8,128)(2,1)S(1)} %all_gather.15.total_ref, bf16[4,32,1280]{2,1,0:T(8,128)(2,1)S(1)} %get-tuple-element.18.keep_ref, ...), custom_call_target="tpu_custom_call" | custom-call | tf_op jit(solution)/shard_map/pallas_call | solution.py:151
  (3 shorter events, 0.0 us)
Async XLA Ops:
  0.6 10.5 %collective-permute-start = (bf16[1024,256]{1,0:T(8,128)(2,1)}, bf16[1024,256]{1,0:T(8,128)(2,1)S(1)}, u32[]{:S(2)}, u32[]{:S(2)}) collective-permute-start(bf16[1024,256]{1,0:T(8,128)(2,1)} %bitcast.13), channel_id=1, source_target_pairs={{0,8},{8,0},{1,9},{9,1},{2,10},{10,2},{3,11},{11,3},{4,12},{12,4},... | collective-permute-start | bytes 1572872 | tf_op jit(solution)/shard_map/ppermute | solution.py:231
  11.2 1.0 copy-start
  30.6 21.7 %copy-start.2 = (bf16[256,1024]{1,0:T(8,128)(2,1)S(1)}, bf16[256,1024]{1,0:T(8,128)(2,1)}, u32[]{:S(2)}) copy-start(bf16[256,1024]{1,0:T(8,128)(2,1)} %grad_ref.1) | copy-start | bytes 1572868
  47.0 5.3 %copy-start.1 = (bf16[256,1024]{1,0:T(8,128)(2,1)S(1)}, bf16[256,1024]{1,0:T(8,128)(2,1)}, u32[]{:S(2)}) copy-start(bf16[256,1024]{1,0:T(8,128)(2,1)} %query_ref.1) | copy-start | bytes 1572868
  47.0 5.3 %copy-start.3 = (bf16[256,256]{1,0:T(8,128)(2,1)S(1)}, bf16[256,256]{1,0:T(8,128)(2,1)}, u32[]{:S(2)}) copy-start(bf16[256,256]{1,0:T(8,128)(2,1)} %cont_ref.1) | copy-start | bytes 393220
  72.1 26.8 %collective-permute-start.1 = (bf16[4,32,1280]{2,1,0:T(8,128)(2,1)S(1)}, bf16[4,32,1280]{2,1,0:T(8,128)(2,1)S(1)}, u32[]{:S(2)}, u32[]{:S(2)}) collective-permute-start(bf16[4,32,1280]{2,1,0:T(8,128)(2,1)S(1)} %get-tuple-element.19), channel_id=1, source_target_pairs={{0,1},{1,0},{2,3},{3,2},{4,5},{5,4},{6,7},{7,6},{8,9},{9,8},{10,11... | collective-permute-start | bytes 983048 | tf_op jit(solution)/shard_map/ppermute | solution.py:231
  99.7 17.1 %all-to-all-start.3 = ((bf16[32,16,256]{2,1,0:T(8,128)(2,1)}), bf16[32,16,256]{2,1,0:T(8,128)(2,1)S(1)}, u32[]{:S(2)}, u32[]{:S(2)}) async-start(bf16[32,16,256]{2,1,0:T(8,128)(2,1)} %get-tuple-element.20), calls=%async_computation.3 | async-start | bytes 524288 | tf_op jit(solution)/shard_map/all_to_all | solution.py:225
  106.3 15.3 %collective-permute-start.2 = (bf16[2,32,1280]{2,1,0:T(8,128)(2,1)S(1)}, bf16[2,32,1280]{2,1,0:T(8,128)(2,1)S(1)}, u32[]{:S(2)}, u32[]{:S(2)}) collective-permute-start(bf16[2,32,1280]{2,1,0:T(8,128)(2,1)S(1)} %get-tuple-element.21), channel_id=1, source_target_pairs={{0,2},{1,3},{2,4},{3,5},{4,6},{5,7},{6,0},{7,1},{8,10},{9,11},{10,... | collective-permute-start | bytes 491528 | tf_op jit(solution)/shard_map/ppermute | solution.py:267
  109.4 12.2 %collective-permute-start.3 = (bf16[2,32,1280]{2,1,0:T(8,128)(2,1)S(1)}, bf16[2,32,1280]{2,1,0:T(8,128)(2,1)S(1)}, u32[]{:S(2)}, u32[]{:S(2)}) collective-permute-start(bf16[2,32,1280]{2,1,0:T(8,128)(2,1)S(1)} %get-tuple-element.22), channel_id=1, source_target_pairs={{0,4},{1,5},{2,6},{3,7},{4,0},{5,1},{6,2},{7,3},{8,12},{9,13},{10,... | collective-permute-start | bytes 491528 | tf_op jit(solution)/shard_map/ppermute | solution.py:267
  113.8 7.8 %collective-permute-start.4 = (bf16[2,32,1280]{2,1,0:T(8,128)(2,1)S(1)}, bf16[2,32,1280]{2,1,0:T(8,128)(2,1)S(1)}, u32[]{:S(2)}, u32[]{:S(2)}) collective-permute-start(bf16[2,32,1280]{2,1,0:T(8,128)(2,1)S(1)} %get-tuple-element.23), channel_id=1, source_target_pairs={{0,6},{1,7},{2,0},{3,1},{4,2},{5,3},{6,4},{7,5},{8,14},{9,15},{10,... | collective-permute-start | bytes 491528 | tf_op jit(solution)/shard_map/ppermute | solution.py:267
